TPU v7x, 32 devices: a whole 2x2x4 slice. The times are simulated.
32 devices in a mesh: kz: 4 (over y, x), gx: 8 (over z, core).
Axes of the slice: x: 2, y: 2, z: 4, core: 2. Of those that a mesh axis runs over, the one named last changes fastest.
Arguments:
- kspace_lines: bfloat16 [16, 4, 32, 2, 512], P(None, 'kz', 'gx'), may hold values from -6 to 6
- acquired_at: int32 [4, 32], P('kz'), may hold values from 0 to 5
- ky_start: int32 [6], replicated, may hold values from -2 to 0, as said below
- kz_start: int32 [6], replicated, may hold values from -1 to 0, as said below
- kernels: bfloat16 [2, 6, 16, 6, 32], replicated, may hold values from -0.3125 to 0.3125
Outputs:
- filled: bfloat16 [2, 512, 16, 8, 96], P(None, 'gx', None, 'kz')
Inputs may be any that keep to these rules, and one draw needn't show every extreme that they name: acquired_at[b, a] = 2 ry + rz names the acquired position of the cell, with ky = 3 a + ry and kz = 2 b + rz. `ky_start`: each of -2, -1 and 0 appears exactly twice. `kz_start`: each of -1 and 0 appears exactly three times.
All inputs are finite; a program needn't handle non-finite values.
Results may differ from a plain program's by a relative error of at most 0.0057.
Values may be sent and summed in bfloat16 or wider, within the bound.
A program may use at most 64 MiB of HBM per device.

v0:
```python
import math

import jax
import jax.numpy as jnp
from jax import lax
from jax.sharding import PartitionSpec as P


def with_halo(cells, sides, width):
    for axis, dim in sides:
        count = lax.axis_size(axis)
        ends = count - 1
        head = lax.slice_in_dim(cells, 0, width, axis=dim)
        tail = lax.slice_in_dim(cells, cells.shape[dim] - width, cells.shape[dim], axis=dim)
        cells = jnp.concatenate(
            [
                lax.ppermute(tail, axis, [(i, (i + 1) % count) for i in range(ends)]),
                cells,
                lax.ppermute(head, axis, [((i + 1) % count, i) for i in range(ends)]),
            ],
            axis=dim,
        )
    return cells


def readout_matrix(extent):
    wave_index = jnp.arange(extent, dtype=jnp.int32)
    phase_angle = (wave_index[:, None] * wave_index[None, :] % extent).astype(jnp.float32) * (
        2.0 * math.pi / extent
    )
    cosine = jnp.cos(phase_angle) / math.sqrt(extent)
    sine_part = jnp.sin(phase_angle) / math.sqrt(extent)
    from_real = jnp.stack([cosine, sine_part], axis=1)
    from_imag = jnp.stack([-sine_part, cosine], axis=1)
    return jnp.stack([from_real, from_imag], axis=0).astype(jnp.bfloat16)


def conjugate_flip(blocks):
    flipped = blocks[:, :, :, ::-1, ::-1]
    return jnp.concatenate([flipped[0:1], -flipped[1:2]], axis=0)


def complex_weights(kernels):
    real_part = kernels[0]
    imag_part = kernels[1]
    to_real = jnp.stack([real_part, -imag_part], axis=3)
    to_imag = jnp.stack([imag_part, real_part], axis=3)
    return jnp.stack([to_real, to_imag], axis=1)


def fill_grid(padded, actual, weights, acquired_at, ky_start, kz_start):
    kz_cells = actual.shape[3]
    ky_cells = actual.shape[4]
    filled = []
    for target in range(6):
        pieces = []
        for kz_point in range(2):
            kz_from = kz_start[target] + 1 + kz_point
            plane_rows = lax.dynamic_slice_in_dim(padded, kz_from, kz_cells, axis=3)
            for ky_point in range(3):
                ky_from = ky_start[target] + 2 + ky_point
                pieces.append(lax.dynamic_slice_in_dim(plane_rows, ky_from, ky_cells, axis=4))
        source = jnp.stack(pieces, axis=0)
        estimate = jnp.einsum(
            "scpqh,pqxhba->sxcba", weights[target], source, preferred_element_type=jnp.float32
        )
        chosen = jnp.where(acquired_at == target, actual.astype(jnp.float32), estimate)
        filled.append(chosen.astype(jnp.bfloat16))
    stacked = jnp.stack(filled, axis=0).reshape((3, 2) + actual.shape)
    reordered = jnp.transpose(stacked, (2, 3, 4, 5, 1, 6, 0))
    return reordered.reshape(
        actual.shape[0], actual.shape[1], actual.shape[2], 2 * kz_cells, 3 * ky_cells
    )


def local(kspace_lines, acquired_at, ky_start, kz_start, kernels):
    spectra = jnp.einsum(
        "cbaqk,qksx->sxcba",
        kspace_lines,
        readout_matrix(kspace_lines.shape[4]),
        preferred_element_type=jnp.float32,
    ).astype(jnp.bfloat16)
    planes = lax.all_to_all(spectra, "gx", split_axis=1, concat_axis=4, tiled=True)
    kz_slabs = lax.all_to_all(planes, "kz", split_axis=2, concat_axis=3, tiled=True)
    virtual = lax.all_to_all(
        conjugate_flip(kz_slabs), "kz", split_axis=3, concat_axis=2, tiled=True
    )
    channels = jnp.concatenate([planes, virtual], axis=2)
    padded = with_halo(channels, (("kz", 3),), 1)
    padded = jnp.pad(padded, ((0, 0), (0, 0), (0, 0), (0, 0), (2, 2)))
    return fill_grid(padded, planes, complex_weights(kernels), acquired_at, ky_start, kz_start)


def solution(mesh):
    placed = (P(None, "kz", "gx", None, None), P("kz", None), P(), P(), P())
    return jax.shard_map(
        local,
        mesh=mesh,
        in_specs=placed,
        out_specs=P(None, "gx", None, "kz", None),
        check_vma=False,
    )
```

profile of v0, /device:TPU:0, one launch (start us, length us, event | category | flops | bytes accessed | tf_op | source)
XLA Modules:
  0.0 102.5 jit_solution(4896297500615457863)
XLA Ops:
  0.0 0.0 copy-start.4
  0.0 4.4 %negate_convert_fusion = (bf16[512,1,512]{2,0,1:T(8,128)(2,1)S(1)}, bf16[512,1,512]{2,0,1:T(8,128)(2,1)S(1)}) fusion(), kind=kLoop, calls=%fused_computation.63 | loop fusion | flops 4980736 | bytes 1048576 | tf_op jit(solution)/shard_map/convert.3
  4.4 4.0 %fusion.110 = bf16[512,1,512]{2,0,1:T(8,128)(2,1)S(1)} fusion(), kind=kLoop, calls=%fused_computation.69 | loop fusion | flops 4194304 | bytes 524288 | tf_op jit(solution)/shard_map/convert.7
  8.4 0.2 maximum_bitcast_fusion.8
  8.6 0.0 copy-done.4
  8.6 0.0 copy-start
  8.6 0.4 fusion.103
  9.1 0.7 copy.23
  9.7 1.7 %reshape.296 = bf16[8,2,4096]{2,1,0:T(2,128)(2,1)} reshape(bf16[512,1,2,4,16]{4,3,2,1,0:T(4,128)(2,1)S(1)} %bitcast.461) | data formatting | bytes 262144
  11.5 6.3 %all-to-all-start = ((bf16[8,2,4096]{2,1,0:T(2,128)(2,1)}), bf16[8,2,4096]{2,1,0:T(2,128)(2,1)S(1)}, u32[]{:S(2)}, u32[]{:S(2)}) async-start(bf16[8,2,4096]{2,1,0:T(2,128)(2,1)} %reshape.296), calls=%async_computation | async-start | bytes 262144 | tf_op jit(solution)/shard_map/all_to_all | solution.py:83
  17.8 0.0 copy-done
  17.9 6.7 %all-to-all-done = bf16[8,2,4096]{2,1,0:T(2,128)(2,1)S(1)} async-done(((bf16[8,2,4096]{2,1,0:T(2,128)(2,1)}), bf16[8,2,4096]{2,1,0:T(2,128)(2,1)S(1)}, u32[]{:S(2)}, u32[]{:S(2)}) %all-to-all-start) | async-done | bytes 131104 | tf_op jit(solution)/shard_map/all_to_all | solution.py:83
  24.6 0.7 reshape.297
  25.3 0.0 copy-start.1
  25.3 0.6 copy.24
  25.9 0.2 copy.53
  26.2 0.9 reshape.298
  27.1 3.7 %all-to-all-start.1 = ((bf16[4,2,8192]{2,1,0:T(2,128)(2,1)}), bf16[4,2,8192]{2,1,0:T(2,128)(2,1)S(1)}, u32[]{:S(2)}, u32[]{:S(2)}) async-start(bf16[4,2,8192]{2,1,0:T(2,128)(2,1)} %reshape.298), calls=%async_computation.1 | async-start | bytes 262144 | tf_op jit(solution)/shard_map/all_to_all | solution.py:84
  30.8 0.0 copy-start.2
  30.8 0.1 maximum_bitcast_fusion.11
  30.9 0.0 copy-start.3
  30.9 4.9 %all-to-all-done.1 = bf16[4,2,8192]{2,1,0:T(2,128)(2,1)S(1)} async-done(((bf16[4,2,8192]{2,1,0:T(2,128)(2,1)}), bf16[4,2,8192]{2,1,0:T(2,128)(2,1)S(1)}, u32[]{:S(2)}, u32[]{:S(2)}) %all-to-all-start.1) | async-done | bytes 131104 | tf_op jit(solution)/shard_map/all_to_all | solution.py:84
  35.8 0.2 reshape.299
  36.1 0.2 copy.52
  36.3 0.1 slice_bitcast_fusion.3
  36.4 0.1 reverse_negate_fusion
  36.5 0.2 fusion.141
  36.7 0.9 reshape.300
  37.6 3.3 %all-to-all-start.2 = ((bf16[4,2,8192]{2,1,0:T(2,128)(2,1)}), bf16[4,2,8192]{2,1,0:T(2,128)(2,1)S(1)}, u32[]{:S(2)}, u32[]{:S(2)}) async-start(bf16[4,2,8192]{2,1,0:T(2,128)(2,1)} %reshape.300), calls=%async_computation.2 | async-start | bytes 262144 | tf_op jit(solution)/shard_map/all_to_all | solution.py:85
  41.0 0.0 copy-done.1
  41.0 0.7 fusion.139
  41.7 4.3 %all-to-all-done.2 = bf16[4,2,8192]{2,1,0:T(2,128)(2,1)S(1)} async-done(((bf16[4,2,8192]{2,1,0:T(2,128)(2,1)}), bf16[4,2,8192]{2,1,0:T(2,128)(2,1)S(1)}, u32[]{:S(2)}, u32[]{:S(2)}) %all-to-all-start.2) | async-done | bytes 131104 | tf_op jit(solution)/shard_map/all_to_all | solution.py:85
  46.0 0.2 reshape.301
  46.2 0.1 bitcast_bitcast_fusion
  46.3 0.1 copy.28
  46.4 0.1 pad_maximum_fusion
  46.5 2.9 %collective-permute-start = (bf16[2,64,32,1,32]{1,2,0,4,3:T(8,128)(2,1)S(1)}, bf16[2,64,32,1,32]{1,2,0,4,3:T(8,128)(2,1)S(1)}, u32[]{:S(2)}, u32[]{:S(2)}) collective-permute-start(bf16[2,64,32,1,32]{1,2,0,4,3:T(8,128)(2,1)S(1)} %pad_maximum_fusion), channel_id=1, source_target_pairs={{0,8},{8,16},{16,24},{1,9},{9,17},{17,25},{2,10},{10,18},{18,26},{... | collective-permute-start | bytes 786440 | tf_op jit(solution)/shard_map/ppermute | solution.py:17
  49.4 1.5 %collective-permute-start.1 = (bf16[2,64,32,1,32]{1,2,0,4,3:T(8,128)(2,1)S(1)}, bf16[2,64,32,1,32]{1,2,0,4,3:T(8,128)(2,1)S(1)}, u32[]{:S(2)}, u32[]{:S(2)}) collective-permute-start(bf16[2,64,32,1,32]{1,2,0,4,3:T(8,128)(2,1)S(1)} %pad_maximum_fusion), channel_id=1, source_target_pairs={{8,0},{16,8},{24,16},{9,1},{17,9},{25,17},{10,2},{18,10},{26,18},{... | collective-permute-start | bytes 786440 | tf_op jit(solution)/shard_map/ppermute | solution.py:19
  50.9 0.0 copy-done.2
  50.9 0.7 fusion.140
  89.3 0.0 copy-done.3
  89.3 0.0 collective-permute-done
  89.3 0.0 collective-permute-done.1
  89.3 0.5 select_maximum_fusion
  89.8 1.0 bitcast_dynamic-update-slice_fusion.5
  90.8 0.9 bitcast_dynamic-update-slice_fusion.4
  91.8 0.9 bitcast_dynamic-update-slice_fusion.3
  92.7 0.9 bitcast_dynamic-update-slice_fusion.2
  93.6 0.9 bitcast_dynamic-update-slice_fusion.1
  94.5 0.9 bitcast_dynamic-update-slice_fusion
  95.5 0.6 fusion.69
  96.1 0.7 fusion.75
  96.8 0.7 fusion.81
  97.5 0.7 fusion.87
  98.2 0.7 fusion.93
  98.9 0.7 fusion.99
  99.6 0.3 copy.30
  99.8 2.7 %copy.31 = bf16[2,64,16,2,96]{4,3,2,1,0:T(2,128)(2,1)} copy(bf16[2,64,16,2,96]{1,2,4,3,0:T(8,128)(2,1)S(1)} %bitcast.459) | data formatting | bytes 1572864 | tf_op jit(solution)/shard_map/reshape | solution.py:71
  (4 shorter events, 0.1 us)
Async XLA Ops:
  0.0 8.6 %copy-start.4 = (bf16[16,1,4,2,512]{4,3,2,1,0:T(2,128)(2,1)S(1)}, bf16[16,1,4,2,512]{4,3,2,1,0:T(2,128)(2,1)}, u32[]{:S(2)}) copy-start(bf16[16,1,4,2,512]{4,3,2,1,0:T(2,128)(2,1)} %param.5) | copy-start | bytes 393220
  8.6 9.2 %copy-start = (bf16[2,6,16,6,32]{4,2,3,1,0:T(8,128)(2,1)S(1)}, bf16[2,6,16,6,32]{4,2,3,1,0:T(8,128)(2,1)}, u32[]{:S(2)}) copy-start(bf16[2,6,16,6,32]{4,2,3,1,0:T(8,128)(2,1)} %param.9) | copy-start | bytes 221188
  11.5 13.1 %all-to-all-start = ((bf16[8,2,4096]{2,1,0:T(2,128)(2,1)}), bf16[8,2,4096]{2,1,0:T(2,128)(2,1)S(1)}, u32[]{:S(2)}, u32[]{:S(2)}) async-start(bf16[8,2,4096]{2,1,0:T(2,128)(2,1)} %reshape.296), calls=%async_computation | async-start | bytes 262144 | tf_op jit(solution)/shard_map/all_to_all | solution.py:83
  25.3 15.7 %copy-start.1 = (s32[6]{0:T(128)S(1)}, s32[6]{0:T(128)}, u32[]{:S(2)}) copy-start(s32[6]{0:T(128)} %param.7) | copy-start | bytes 76
  27.1 8.7 %all-to-all-start.1 = ((bf16[4,2,8192]{2,1,0:T(2,128)(2,1)}), bf16[4,2,8192]{2,1,0:T(2,128)(2,1)S(1)}, u32[]{:S(2)}, u32[]{:S(2)}) async-start(bf16[4,2,8192]{2,1,0:T(2,128)(2,1)} %reshape.298), calls=%async_computation.1 | async-start | bytes 262144 | tf_op jit(solution)/shard_map/all_to_all | solution.py:84
  30.8 20.0 %copy-start.2 = (s32[6]{0:T(128)S(1)}, s32[6]{0:T(128)}, u32[]{:S(2)}) copy-start(s32[6]{0:T(128)} %param.8) | copy-start | bytes 76
  30.9 58.4 %copy-start.3 = (s32[1,32]{1,0:T(1,128)S(1)}, s32[1,32]{1,0:T(1,128)}, u32[]{:S(2)}) copy-start(s32[1,32]{1,0:T(1,128)} %param.6) | copy-start | bytes 388
  37.6 8.3 %all-to-all-start.2 = ((bf16[4,2,8192]{2,1,0:T(2,128)(2,1)}), bf16[4,2,8192]{2,1,0:T(2,128)(2,1)S(1)}, u32[]{:S(2)}, u32[]{:S(2)}) async-start(bf16[4,2,8192]{2,1,0:T(2,128)(2,1)} %reshape.300), calls=%async_computation.2 | async-start | bytes 262144 | tf_op jit(solution)/shard_map/all_to_all | solution.py:85
  46.5 42.8 %collective-permute-start = (bf16[2,64,32,1,32]{1,2,0,4,3:T(8,128)(2,1)S(1)}, bf16[2,64,32,1,32]{1,2,0,4,3:T(8,128)(2,1)S(1)}, u32[]{:S(2)}, u32[]{:S(2)}) collective-permute-start(bf16[2,64,32,1,32]{1,2,0,4,3:T(8,128)(2,1)S(1)} %pad_maximum_fusion), channel_id=1, source_target_pairs={{0,8},{8,16},{16,24},{1,9},{9,17},{17,25},{2,10},{10,18},{18,26},{... | collective-permute-start | bytes 786440 | tf_op jit(solution)/shard_map/ppermute | solution.py:17
  49.4 39.9 %collective-permute-start.1 = (bf16[2,64,32,1,32]{1,2,0,4,3:T(8,128)(2,1)S(1)}, bf16[2,64,32,1,32]{1,2,0,4,3:T(8,128)(2,1)S(1)}, u32[]{:S(2)}, u32[]{:S(2)}) collective-permute-start(bf16[2,64,32,1,32]{1,2,0,4,3:T(8,128)(2,1)S(1)} %pad_maximum_fusion), channel_id=1, source_target_pairs={{8,0},{16,8},{24,16},{9,1},{17,9},{25,17},{10,2},{18,10},{26,18},{... | collective-permute-start | bytes 786440 | tf_op jit(solution)/shard_map/ppermute | solution.py:19
where the time goes:
time: 104 us; the launch traced here: 102 us
  between operations  38.1 us (37%)
  starting transfers between devices  17.7 us (17%)
  local copies, waits for them, and re-layouts  16.7 us (16%)
  waiting for transfers between devices  15.9 us (15%)
  other arithmetic  9.59 us (9%)
  matrix products  4.48 us (4%)
    unnamed x21, local copies, waits for them, and re-layouts  9.36 us
    another operation x2, other arithmetic  8.39 us
    all_to_all x1, waiting for transfers between devices, local(): lax.all_to_all(spectra, 'gx', split_axis=1, concat_axis=4, tiled=True)  6.72 us
    all_to_all x1, starting transfers between devices, local(): lax.all_to_all(spectra, 'gx', split_axis=1, concat_axis=4, tiled=True)  6.33 us
    all_to_all x1, waiting for transfers between devices, local(): lax.all_to_all(planes, 'kz', split_axis=2, concat_axis=3, tiled=True)  4.91 us
    all_to_all x1, waiting for transfers between devices, local(): lax.all_to_all(conjugate_flip(kz_slabs), 'kz', split_axis=3, concat_axis=...  4.29 us
    dot_general x6, matrix products, fill_grid(): jnp.einsum('scpqh,pqxhba->sxcba', weights[target], source, preferred_elem...  4.04 us
    all_to_all x1, starting transfers between devices, local(): lax.all_to_all(planes, 'kz', split_axis=2, concat_axis=3, tiled=True)  3.72 us
  transfers between devices with their start and end apart: 5, of which 3 were waited for; matrix products, arithmetic and copies ran while one was open for 1% of the time, Pallas kernels for 0%

commit v1 on v0

v1 whole, which is shorter than its diff:
```python
import functools
import math

import jax
import jax.numpy as jnp
import ml_dtypes
import numpy as np
from jax import lax
from jax.experimental import pallas as pl
from jax.experimental.pallas import tpu as pltpu
from jax.sharding import PartitionSpec as P

BF16 = ml_dtypes.bfloat16
MESH = pl.DeviceIdType.MESH
GROUP = 4
EDGE = 4
LIMIT = 50 * 1024 * 1024


def readout_table(extent):
    index = np.arange(extent)
    angle = (index[:, None] * index[None, :] % extent) * (2.0 * math.pi / extent)
    return np.concatenate([np.cos(angle), np.sin(angle)], axis=1).astype(np.float64) / math.sqrt(extent)


def line_order(coils, cells):
    order = np.zeros((2, cells, 2, coils, coils, cells, 2), np.float32)
    for c in range(coils):
        for a in range(cells):
            order[0, a, 0, c, c, a, 0] = 1
            order[0, a, 1, c, c, a, 1] = 1
            order[1, a, 0, c, c, a, 1] = -1
            order[1, a, 1, c, c, a, 0] = 1
    return order.reshape(4 * cells * coils, 2 * coils * cells).astype(BF16)


def slab_order(values):
    order = np.zeros((GROUP, GROUP, values, GROUP, GROUP, values), np.float32)
    for b in range(GROUP):
        for a in range(GROUP):
            for v in range(values):
                order[b, a, v, a, b, v] = 1
    return order.reshape(GROUP * GROUP * values, -1).astype(BF16)


def weight_lanes(coils):
    lanes = np.zeros((2, 2, coils, 2, 2, GROUP, 2, coils), np.float32)
    for v in range(2):
        sign = -1 if v else 1
        for c in range(coils):
            lanes[0, v, c, 0, v, :, 0, c] = 1
            lanes[1, v, c, 0, v, :, 1, c] = -sign
            lanes[1, v, c, 1, v, :, 0, c] = 1
            lanes[0, v, c, 1, v, :, 1, c] = sign
    return lanes.reshape(2, 2 * coils, -1).astype(BF16)


def row_order(coils):
    values = 2 * coils
    order = np.zeros((4, values, 2, 7 * values), np.float32)
    for n in range(values):
        for rz in range(2):
            for ry in range(3):
                order[ry, n, rz, (ry * 2 + rz) * values + n] = 1
            order[3, n, rz, 6 * values + n] = 1
    return order.reshape(8 * values, 7 * values).astype(BF16)


def lane_order(cells, width):
    each = 128 // cells
    order = np.zeros((3, each, cells, each, width), np.float32)
    for ry in range(3):
        for x in range(each):
            for a in range(cells):
                order[ry, x, a, x, 3 * a + ry] = 1
    return order.reshape(3 * 128, each * width).astype(BF16)


def nt(left, right):
    return lax.dot_general(left, right, (((1,), (1,)), ((), ())), preferred_element_type=jnp.float32)


def gather_kernel(nkz, ngx, table, lines, order, planes, spectra, send_x, recv_x, send_z, recv_z):
    b, g = lax.axis_index("kz"), lax.axis_index("gx")
    barrier = pltpu.get_barrier_semaphore()
    for k in range(1, ngx):
        pl.semaphore_signal(barrier, inc=1, device_id=(b, lax.rem(g + k, ngx)), device_id_type=MESH)
    for j in range(1, nkz):
        pl.semaphore_signal(barrier, inc=1, device_id=(lax.rem(b + j, nkz), g), device_id_type=MESH)

    count = lines.shape[0]
    both = jnp.dot(order[...], lines[...], preferred_element_type=jnp.float32).astype(jnp.bfloat16)
    right = jnp.concatenate([both[:count], both[count:]], axis=1)
    values = nt(table[...], right).astype(jnp.bfloat16)
    spectra[...] = values.reshape(spectra.shape)
    planes[b, g] = spectra[g]

    pl.semaphore_wait(barrier, ngx + nkz - 2)
    along_x, along_z = {}, {}
    for k in range(1, ngx):
        to = lax.rem(g + k, ngx)
        along_x[k] = pltpu.make_async_remote_copy(
            src_ref=spectra.at[to], dst_ref=planes.at[b, g], send_sem=send_x.at[k],
            recv_sem=recv_x.at[k], device_id=(b, to), device_id_type=MESH)
        along_x[k].start()
    for k in range(ngx):
        if k:
            along_x[k].wait_recv()
        source = lax.rem(g + ngx - k, ngx)
        for j in range(1, nkz):
            along_z[j, k] = pltpu.make_async_remote_copy(
                src_ref=planes.at[b, source], dst_ref=planes.at[b, source], send_sem=send_z.at[j, k],
                recv_sem=recv_z.at[j, k], device_id=(lax.rem(b + j, nkz), g), device_id_type=MESH)
            along_z[j, k].start()
    for copy in along_z.values():
        copy.wait_recv()
    for copy in list(along_x.values()) + list(along_z.values()):
        copy.wait_send()


def fill_kernel(nkz, ky_start, kz_start, planes, parts, acquired, to_slabs, to_lanes, to_rows, to_ky,
                out, near, far, natural, weights):
    b = lax.axis_index("kz")
    _, ngx, xs, lanes = planes.shape
    cells = ngx * GROUP
    pitch = cells + 2 * EDGE
    sets = nkz // GROUP
    coils = parts.shape[3]
    values = 2 * coils
    f32, bf16 = jnp.float32, jnp.bfloat16

    terms = (
        jnp.dot(parts[0].reshape(36 * coils, values), to_lanes[0], preferred_element_type=f32)
        + jnp.dot(parts[1].reshape(36 * coils, values), to_lanes[1], preferred_element_type=f32)
    )
    lane = lax.broadcasted_iota(jnp.int32, (coils, 128), 1)
    slab = lane // values
    for t in range(6):
        for v in range(2):
            for part in range(sets):
                cell = slab + part * GROUP
                if v:
                    cell = nkz - 1 - cell
                point = cell - b - kz_start[t]
                for s in range(2):
                    column = (s * 2 + v) * 128
                    rows = []
                    for i in range(3):
                        at = (t * 6 + i) * coils
                        first = terms[at : at + coils, column : column + 128]
                        second = terms[at + 3 * coils : at + 4 * coils, column : column + 128]
                        rows.append(jnp.where(point == 0, first, jnp.where(point == 1, second, 0.0)))
                    for d in range(-2, 3):
                        total = jnp.zeros((coils, 128), f32)
                        for i in range(3):
                            if -2 <= d - i <= 0:
                                here = jnp.full((coils, 128), ky_start[t], jnp.int32) == d - i
                                total = jnp.where(here, rows[i], total)
                        where = ((v * 5 + d + 2) * sets + part) * 128
                        natural[(t * 2 + s) * coils : (t * 2 + s + 1) * coils, where : where + 128] = total.astype(bf16)
    natural[12 * coils :, :] = jnp.zeros((values, natural.shape[1]), bf16)
    row = lax.broadcasted_iota(jnp.int32, (values, 128), 0)
    wide = lax.broadcasted_iota(jnp.int32, (values, 128), 1)
    for part in range(sets):
        same = (b - part * GROUP) * values + row == wide
        where = (2 * sets + part) * 128
        natural[12 * coils :, where : where + 128] = jnp.where(same, 1.0, 0.0).astype(bf16)
    weights[...] = jnp.dot(to_rows[...], natural[...], preferred_element_type=f32).astype(bf16)

    for x in range(sets * xs):
        for buffer in (near, far):
            buffer[x * pitch : x * pitch + EDGE, :] = jnp.zeros((EDGE, buffer.shape[1]), f32)
            buffer[(x + 1) * pitch - EDGE : (x + 1) * pitch, :] = jnp.zeros((EDGE, buffer.shape[1]), f32)
    for part in range(sets):
        for g in range(ngx):
            block = jnp.concatenate([planes[part * GROUP + n, g] for n in range(GROUP)], axis=1)
            turned = jnp.dot(block, to_slabs[...], preferred_element_type=f32)
            for n in range(GROUP):
                a = g * GROUP + n
                piece = turned[:, n * 128 : (n + 1) * 128]
                base = part * xs * pitch + EDGE
                near[pl.ds(base + a, xs, stride=pitch), :] = piece
                far[pl.ds(base + cells - 1 - a, xs, stride=pitch), :] = piece

    each = 128 // cells
    width = to_ky.shape[1] // each
    step = 2 * each
    odd = lax.broadcasted_iota(jnp.int32, (2 * values, 2 * 128), 0) % 2
    for start in range(0, xs, step):
        pieces = []
        for buffer in (near, far):
            for d in range(-2, 3):
                for part in range(sets):
                    rows = [(part * xs + x) * pitch + EDGE + d for x in range(start, start + step)]
                    pieces.append(jnp.concatenate([buffer[r : r + cells, :] for r in rows], axis=0).astype(bf16))
        result = nt(weights[...], jnp.concatenate(pieces, axis=1))
        actual = result[6 * values :]
        chosen = [
            jnp.where(acquired[...] == odd + 2 * ry, actual, result[ry * 2 * values : (ry + 1) * 2 * values]).astype(bf16)
            for ry in range(3)
        ]
        for half in range(2):
            line = jnp.concatenate([c[:, half * 128 : (half + 1) * 128] for c in chosen], axis=1)
            spread = jnp.dot(line, to_ky[...], preferred_element_type=f32).astype(bf16)
            for n in range(each):
                x = start + half * each + n
                for s in range(2):
                    out[s * xs + x] = spread[s * values : (s + 1) * values, n * width : n * width + 3 * cells]


def local(kspace_lines, acquired_at, ky_start, kz_start, kernels):
    nkz, ngx = lax.axis_size("kz"), lax.axis_size("gx")
    coils, _, own, _, extent = kspace_lines.shape
    xs, cells = extent // ngx, ngx * own
    assert own == GROUP and nkz % GROUP == 0 and 2 * coils * GROUP == 128 and 128 % cells == 0
    vmem = pl.BlockSpec(memory_space=pltpu.VMEM)
    smem = pl.BlockSpec(memory_space=pltpu.SMEM)
    table = jnp.asarray(readout_table(extent).astype(BF16))
    planes = pl.pallas_call(
        functools.partial(gather_kernel, nkz, ngx),
        out_shape=jax.ShapeDtypeStruct((nkz, ngx, xs, 128), jnp.bfloat16),
        in_specs=[vmem] * 3,
        out_specs=vmem,
        scratch_shapes=[
            pltpu.VMEM((ngx, xs, 128), jnp.bfloat16),
            pltpu.SemaphoreType.DMA((ngx,)),
            pltpu.SemaphoreType.DMA((ngx,)),
            pltpu.SemaphoreType.DMA((nkz, ngx)),
            pltpu.SemaphoreType.DMA((nkz, ngx)),
        ],
        compiler_params=pltpu.CompilerParams(
            collective_id=0, has_side_effects=True, vmem_limit_bytes=LIMIT),
    )(table, kspace_lines.reshape(coils * own * 2, extent), jnp.asarray(line_order(coils, own)))

    each = 128 // cells
    width = -(-3 * cells // 128) * 128
    sets = nkz // GROUP
    taps = 10 * 128 * sets
    pitch = cells + 2 * EDGE
    filled = pl.pallas_call(
        functools.partial(fill_kernel, nkz),
        out_shape=jax.ShapeDtypeStruct((2 * xs, 2 * coils, 3 * cells), jnp.bfloat16),
        in_specs=[smem, smem] + [vmem] * 7,
        out_specs=vmem,
        scratch_shapes=[
            pltpu.VMEM((sets * xs * pitch, 128), jnp.float32),
            pltpu.VMEM((sets * xs * pitch, 128), jnp.float32),
            pltpu.VMEM((14 * coils, taps), jnp.bfloat16),
            pltpu.VMEM((16 * coils, taps), jnp.bfloat16),
        ],
        compiler_params=pltpu.CompilerParams(vmem_limit_bytes=LIMIT),
    )(
        ky_start, kz_start, planes, jnp.transpose(kernels, (0, 1, 3, 2, 4)),
        jnp.tile(acquired_at, (1, 2 * each)), jnp.asarray(slab_order(2 * coils)),
        jnp.asarray(weight_lanes(coils)), jnp.asarray(row_order(coils)), jnp.asarray(lane_order(cells, width)),
    )
    return filled.reshape(2, xs, coils, 2, 3 * cells)


def solution(mesh):
    placed = (P(None, "kz", "gx", None, None), P("kz", None), P(), P(), P())
    return jax.shard_map(
        local,
        mesh=mesh,
        in_specs=placed,
        out_specs=P(None, "gx", None, "kz", None),
        check_vma=False,
    )
```

time: 104 us -> 27.9 us (0.27); the launches traced: 102 us -> 27.7 us
  between operations: 38.1 us -> 0.11 us
  Pallas kernels: 0 us -> 24.6 us
  starting transfers between devices: 17.7 us -> 0 us
  waiting for transfers between devices: 15.9 us -> 0 us
  local copies, waits for them, and re-layouts: 16.7 us -> 2.99 us
  other arithmetic: 9.59 us -> 0 us
  matrix products: 4.48 us -> 0 us
    pallas_call x0 -> x2, Pallas kernels: none -> 24.6 us  [the longest x1 15.8 us: local(): pl.pallas_call(functools.partial(gather_kernel, nkz, ngx), out_shape=jax....]
    all_to_all x3 -> x0, waiting for transfers between devices: 15.9 us -> none  [the longest x1 6.72 us: local(): lax.all_to_all(spectra, 'gx', split_axis=1, concat_axis=4, tiled=True)]
    all_to_all x3 -> x0, starting transfers between devices: 13.4 us -> none  [the longest x1 6.33 us: local(): lax.all_to_all(spectra, 'gx', split_axis=1, concat_axis=4, tiled=True)]
    another operation x4 -> x0, other arithmetic: 8.66 us -> none
    unnamed x21 -> x20, local copies, waits for them, and re-layouts: 9.36 us -> 1.91 us
    dot_general x7 -> x0, matrix products: 4.48 us -> none  [the longest x6 4.04 us: fill_grid(): jnp.einsum('scpqh,pqxhba->sxcba', weights[target], source, preferred_elem...]
    ppermute x2 -> x0, starting transfers between devices: 4.33 us -> none  [the longest x1 2.85 us: with_halo(): lax.ppermute(tail, axis, [(i, (i + 1) % count) for i in range(ends)])]
    reshape x2 -> x1, local copies, waits for them, and re-layouts: 2.92 us -> 0.99 us  [local(): kspace_lines.reshape(coils * own * 2, extent)]
  transfers between devices with their start and end apart: 5 -> 0, of which waited for: 3 -> 0; matrix products, arithmetic and copies ran while one was open for 1% -> 0% of each run, Pallas kernels for 0% -> 0%
where the time goes in v1:
time: 27.9 us; the launch traced here: 27.7 us
  Pallas kernels  24.6 us (88%)
  local copies, waits for them, and re-layouts  2.99 us (11%)
    pallas_call x1, Pallas kernels, local(): pl.pallas_call(functools.partial(gather_kernel, nkz, ngx), out_shape=jax....  15.8 us
    pallas_call x1, Pallas kernels, local(): pl.pallas_call(functools.partial(fill_kernel, nkz), out_shape=jax.ShapeDt...  8.82 us
    unnamed x20, local copies, waits for them, and re-layouts  1.91 us
    reshape x1, local copies, waits for them, and re-layouts, local(): kspace_lines.reshape(coils * own * 2, extent)  0.99 us

profile of v1, /device:TPU:0, one launch (start us, length us, event | category | flops | bytes accessed | tf_op | source)
XLA Modules:
  0.0 27.7 jit_solution(15030892050948638389)
XLA Ops:
  0.0 0.0 copy-start.9
  0.0 0.7 %copy-done.9 = s32[1,32]{1,0:T(1,128)S(1)} copy-done((s32[1,32]{1,0:T(1,128)S(1)}, s32[1,32]{1,0:T(1,128)}, u32[]{:S(2)}) %copy-start.9) | copy-done | bytes 152
  0.7 0.1 tile.13.acquired
  0.7 0.0 copy-start.5
  0.7 1.0 %reshape.12.lines = bf16[128,512]{1,0:T(8,128)(2,1)S(1)} reshape(bf16[16,1,4,2,512]{4,3,2,1,0:T(2,128)(2,1)} %param.11) | data formatting | bytes 262144 | tf_op jit(solution)/shard_map/reshape | solution.py:233
  1.7 0.0 copy-done.5
  1.7 0.0 copy-start
  1.8 1.2 %copy-done = bf16[512,1024]{1,0:T(8,128)(2,1)S(1)} copy-done((bf16[512,1024]{1,0:T(8,128)(2,1)S(1)}, bf16[512,1024]{1,0:T(8,128)(2,1)}, u32[]{:S(2)}) %copy-start) | copy-done | bytes 1048600
  3.0 0.0 copy-start.1
  3.0 0.0 copy-start.2
  3.0 0.0 copy-start.3
  3.0 0.0 copy-start.4
  3.0 0.0 copy-start.6
  3.0 0.0 copy-start.7
  3.0 0.0 copy-start.8
  3.0 15.8 %shard_map.109.planes = bf16[4,8,64,128]{3,2,1,0:T(8,128)(2,1)S(1)} custom-call(bf16[512,1024]{1,0:T(8,128)(2,1)S(1)} %copy-done, bf16[128,512]{1,0:T(8,128)(2,1)S(1)} %reshape.12.lines, bf16[256,128]{1,0:T(8,128)(2,1)S(1)} %copy-done.5), custom_call_target="tpu_custom_call" | custom-call | tf_op jit(solution)/shard_map/pallas_call | solution.py:219
  18.8 0.0 copy-done.1
  18.8 0.0 copy-done.2
  18.8 0.0 copy-done.3
  18.8 0.0 copy-done.4
  18.8 0.0 copy-done.6
  18.9 0.0 copy-done.7
  18.9 0.0 copy-done.8
  18.9 8.8 %shard_map.110 = bf16[128,32,96]{2,1,0:T(8,128)(2,1)} custom-call(s32[6]{0:T(128)S(1)} %copy-done.7, s32[6]{0:T(128)S(1)} %copy-done.8, bf16[4,8,64,128]{3,2,1,0:T(8,128)(2,1)S(1)} %shard_map.109.planes, bf16[2,6,6,16,32]{4,3,2,1,0:T(8,128)(2,1)S(1)} %bitcast.3, s32[1,256]{1,0:T(1,128)S(1)} %tile.13.acquired, bf16[512,512]{1,0:T(8,128)(2,1)S(1)} %copy-done.1, ...), custom_call_target="tpu_custom_call" | custom-call | tf_op jit(solution)/shard_map/pallas_call | solution.py:240
  (1 shorter events, 0.0 us)
Async XLA Ops:
  0.0 0.7 %copy-start.9 = (s32[1,32]{1,0:T(1,128)S(1)}, s32[1,32]{1,0:T(1,128)}, u32[]{:S(2)}) copy-start(s32[1,32]{1,0:T(1,128)} %param.12) | copy-start | bytes 388
  0.7 1.0 %copy-start.5 = (bf16[256,128]{1,0:T(8,128)(2,1)S(1)}, bf16[256,128]{1,0:T(8,128)(2,1)}, u32[]{:S(2)}) copy-start(bf16[256,128]{1,0:T(8,128)(2,1)} %constant.13.clone.order) | copy-start | bytes 196612
  1.7 1.2 %copy-start = (bf16[512,1024]{1,0:T(8,128)(2,1)S(1)}, bf16[512,1024]{1,0:T(8,128)(2,1)}, u32[]{:S(2)}) copy-start(bf16[512,1024]{1,0:T(8,128)(2,1)} %constant.12.clone.table) | copy-start | bytes 3145732
  3.0 15.8 %copy-start.1 = (bf16[512,512]{1,0:T(8,128)(2,1)S(1)}, bf16[512,512]{1,0:T(8,128)(2,1)}, u32[]{:S(2)}) copy-start(bf16[512,512]{1,0:T(8,128)(2,1)} %constant.14.clone.to_slabs) | copy-start | bytes 1572868
  3.0 15.8 %copy-start.2 = (bf16[384,512]{1,0:T(8,128)(2,1)S(1)}, bf16[384,512]{1,0:T(8,128)(2,1)}, u32[]{:S(2)}) copy-start(bf16[384,512]{1,0:T(8,128)(2,1)} %constant.17.clone.to_ky) | copy-start | bytes 1179652
  3.0 15.8 %copy-start.3 = (bf16[2,6,16,6,32]{4,2,3,1,0:T(8,128)(2,1)S(1)}, bf16[2,6,16,6,32]{4,2,3,1,0:T(8,128)(2,1)}, u32[]{:S(2)}) copy-start(bf16[2,6,16,6,32]{4,2,3,1,0:T(8,128)(2,1)} %param.15) | copy-start | bytes 221188
  3.0 15.9 %copy-start.4 = (bf16[256,224]{1,0:T(8,128)(2,1)S(1)}, bf16[256,224]{1,0:T(8,128)(2,1)}, u32[]{:S(2)}) copy-start(bf16[256,224]{1,0:T(8,128)(2,1)} %constant.16.clone.to_rows) | copy-start | bytes 344068
  3.0 15.9 %copy-start.6 = (bf16[2,32,512]{2,1,0:T(8,128)(2,1)S(1)}, bf16[2,32,512]{2,1,0:T(8,128)(2,1)}, u32[]{:S(2)}) copy-start(bf16[2,32,512]{2,1,0:T(8,128)(2,1)} %constant.15.clone.to_lanes) | copy-start | bytes 196612
  3.0 15.9 %copy-start.7 = (s32[6]{0:T(128)S(1)}, s32[6]{0:T(128)}, u32[]{:S(2)}) copy-start(s32[6]{0:T(128)} %ky_start.1) | copy-start | bytes 76
  3.0 15.9 %copy-start.8 = (s32[6]{0:T(128)S(1)}, s32[6]{0:T(128)}, u32[]{:S(2)}) copy-start(s32[6]{0:T(128)} %kz_start.1) | copy-start | bytes 76

commit v2 on v1

--- a/solution.py
+++ b/solution.py
@@ -80,62 +80,60 @@
     return lax.dot_general(left, right, (((1,), (1,)), ((), ())), preferred_element_type=jnp.float32)
 
 
-def gather_kernel(nkz, ngx, table, lines, order, planes, spectra, send_x, recv_x, send_z, recv_z):
+def gather_kernel(nkz, ngx, ky_start, kz_start, table_hbm, lines, order, parts, to_slabs, to_lanes, to_rows,
+                  near, far, weights, table, planes, spectra, natural, load, send_x, recv_x, send_z, recv_z):
     b, g = lax.axis_index("kz"), lax.axis_index("gx")
     barrier = pltpu.get_barrier_semaphore()
     for k in range(1, ngx):
         pl.semaphore_signal(barrier, inc=1, device_id=(b, lax.rem(g + k, ngx)), device_id_type=MESH)
     for j in range(1, nkz):
         pl.semaphore_signal(barrier, inc=1, device_id=(lax.rem(b + j, nkz), g), device_id_type=MESH)
-
-    count = lines.shape[0]
-    both = jnp.dot(order[...], lines[...], preferred_element_type=jnp.float32).astype(jnp.bfloat16)
+    loading = pltpu.make_async_copy(table_hbm, table, load)
+    loading.start()
+
+    f32, bf16 = jnp.float32, jnp.bfloat16
+    sets = nkz // GROUP
+    coils = parts.shape[3]
+    values = 2 * coils
+    cells = ngx * GROUP
+    pitch = cells + 2 * EDGE
+    xs = spectra.shape[1]
+
+    count = values * GROUP
+    both = jnp.dot(order[...], lines[...].reshape(count, table.shape[0]), preferred_element_type=f32).astype(bf16)
     right = jnp.concatenate([both[:count], both[count:]], axis=1)
-    values = nt(table[...], right).astype(jnp.bfloat16)
-    spectra[...] = values.reshape(spectra.shape)
+    terms = (
+        jnp.dot(parts[0].reshape(36 * coils, values), to_lanes[0], preferred_element_type=f32)
+        + jnp.dot(parts[1].reshape(36 * coils, values), to_lanes[1], preferred_element_type=f32)
+    )
+    loading.wait()
+    spectra[...] = nt(table[...], right).astype(bf16).reshape(spectra.shape)
     planes[b, g] = spectra[g]
 
     pl.semaphore_wait(barrier, ngx + nkz - 2)
     along_x, along_z = {}, {}
+
+    def forward(k):
+        source = lax.rem(g + ngx - k, ngx)
+        for j in range(1, nkz):
+            along_z[j, k] = pltpu.make_async_remote_copy(
+                src_ref=planes.at[b, source], dst_ref=planes.at[b, source], send_sem=send_z.at[j, k],
+                recv_sem=recv_z.at[j, k], device_id=(lax.rem(b + j, nkz), g), device_id_type=MESH)
+            along_z[j, k].start()
+
     for k in range(1, ngx):
         to = lax.rem(g + k, ngx)
         along_x[k] = pltpu.make_async_remote_copy(
             src_ref=spectra.at[to], dst_ref=planes.at[b, g], send_sem=send_x.at[k],
             recv_sem=recv_x.at[k], device_id=(b, to), device_id_type=MESH)
         along_x[k].start()
-    for k in range(ngx):
-        if k:
-            along_x[k].wait_recv()
-        source = lax.rem(g + ngx - k, ngx)
-        for j in range(1, nkz):
-            along_z[j, k] = pltpu.make_async_remote_copy(
-                src_ref=planes.at[b, source], dst_ref=planes.at[b, source], send_sem=send_z.at[j, k],
-                recv_sem=recv_z.at[j, k], device_id=(lax.rem(b + j, nkz), g), device_id_type=MESH)
-            along_z[j, k].start()
-    for copy in along_z.values():
-        copy.wait_recv()
-    for copy in list(along_x.values()) + list(along_z.values()):
-        copy.wait_send()
-
-
-def fill_kernel(nkz, ky_start, kz_start, planes, parts, acquired, to_slabs, to_lanes, to_rows, to_ky,
-                out, near, far, natural, weights):
-    b = lax.axis_index("kz")
-    _, ngx, xs, lanes = planes.shape
-    cells = ngx * GROUP
-    pitch = cells + 2 * EDGE
-    sets = nkz // GROUP
-    coils = parts.shape[3]
-    values = 2 * coils
-    f32, bf16 = jnp.float32, jnp.bfloat16
-
-    terms = (
-        jnp.dot(parts[0].reshape(36 * coils, values), to_lanes[0], preferred_element_type=f32)
-        + jnp.dot(parts[1].reshape(36 * coils, values), to_lanes[1], preferred_element_type=f32)
-    )
+    forward(0)
+
     lane = lax.broadcasted_iota(jnp.int32, (coils, 128), 1)
     slab = lane // values
-    for t in range(6):
+
+    def place(t):
+        here = {n: jnp.full((coils, 128), ky_start[t], jnp.int32) == n for n in (-2, -1, 0)}
         for v in range(2):
             for part in range(sets):
                 cell = slab + part * GROUP
@@ -154,38 +152,57 @@
                         total = jnp.zeros((coils, 128), f32)
                         for i in range(3):
                             if -2 <= d - i <= 0:
-                                here = jnp.full((coils, 128), ky_start[t], jnp.int32) == d - i
-                                total = jnp.where(here, rows[i], total)
+                                total = jnp.where(here[d - i], rows[i], total)
                         where = ((v * 5 + d + 2) * sets + part) * 128
                         natural[(t * 2 + s) * coils : (t * 2 + s + 1) * coils, where : where + 128] = total.astype(bf16)
-    natural[12 * coils :, :] = jnp.zeros((values, natural.shape[1]), bf16)
-    row = lax.broadcasted_iota(jnp.int32, (values, 128), 0)
-    wide = lax.broadcasted_iota(jnp.int32, (values, 128), 1)
-    for part in range(sets):
-        same = (b - part * GROUP) * values + row == wide
-        where = (2 * sets + part) * 128
-        natural[12 * coils :, where : where + 128] = jnp.where(same, 1.0, 0.0).astype(bf16)
+
+    def place_rest():
+        natural[12 * coils :, :] = jnp.zeros((values, natural.shape[1]), bf16)
+        row = lax.broadcasted_iota(jnp.int32, (values, 128), 0)
+        wide = lax.broadcasted_iota(jnp.int32, (values, 128), 1)
+        for part in range(sets):
+            same = (b - part * GROUP) * values + row == wide
+            where = (2 * sets + part) * 128
+            natural[12 * coils :, where : where + 128] = jnp.where(same, 1.0, 0.0).astype(bf16)
+        for x in range(sets * xs):
+            for buffer in (near, far):
+                buffer[x * pitch : x * pitch + EDGE, :] = jnp.zeros((EDGE, 128), f32)
+                buffer[(x + 1) * pitch - EDGE : (x + 1) * pitch, :] = jnp.zeros((EDGE, 128), f32)
+
+    work = [functools.partial(place, t) for t in range(6)] + [place_rest]
+    for k in range(1, ngx):
+        along_x[k].wait_recv()
+        forward(k)
+        if work:
+            work.pop(0)()
     weights[...] = jnp.dot(to_rows[...], natural[...], preferred_element_type=f32).astype(bf16)
 
-    for x in range(sets * xs):
-        for buffer in (near, far):
-            buffer[x * pitch : x * pitch + EDGE, :] = jnp.zeros((EDGE, buffer.shape[1]), f32)
-            buffer[(x + 1) * pitch - EDGE : (x + 1) * pitch, :] = jnp.zeros((EDGE, buffer.shape[1]), f32)
-    for part in range(sets):
-        for g in range(ngx):
-            block = jnp.concatenate([planes[part * GROUP + n, g] for n in range(GROUP)], axis=1)
+    for k in range(ngx):
+        for j in range(1, nkz):
+            along_z[j, k].wait_recv()
+        source = lax.rem(g + ngx - k, ngx)
+        for part in range(sets):
+            block = jnp.concatenate([planes[part * GROUP + n, source] for n in range(GROUP)], axis=1)
             turned = jnp.dot(block, to_slabs[...], preferred_element_type=f32)
             for n in range(GROUP):
-                a = g * GROUP + n
                 piece = turned[:, n * 128 : (n + 1) * 128]
                 base = part * xs * pitch + EDGE
-                near[pl.ds(base + a, xs, stride=pitch), :] = piece
-                far[pl.ds(base + cells - 1 - a, xs, stride=pitch), :] = piece
-
+                near[pl.ds(base + source * GROUP + n, xs, stride=pitch), :] = piece
+                far[pl.ds(base + cells - 1 - n - source * GROUP, xs, stride=pitch), :] = piece
+    for copy in list(along_x.values()) + list(along_z.values()):
+        copy.wait_send()
+
+
+def fill_kernel(sets, xs, near, far, weights, acquired, to_ky, out):
+    cells = acquired.shape[1]
+    values = weights.shape[0] // 8
+    pitch = cells + 2 * EDGE
+    f32, bf16 = jnp.float32, jnp.bfloat16
     each = 128 // cells
     width = to_ky.shape[1] // each
     step = 2 * each
     odd = lax.broadcasted_iota(jnp.int32, (2 * values, 2 * 128), 0) % 2
+    position = jnp.concatenate([acquired[...]] * step, axis=1) - odd
     for start in range(0, xs, step):
         pieces = []
         for buffer in (near, far):
@@ -196,7 +213,7 @@
         result = nt(weights[...], jnp.concatenate(pieces, axis=1))
         actual = result[6 * values :]
         chosen = [
-            jnp.where(acquired[...] == odd + 2 * ry, actual, result[ry * 2 * values : (ry + 1) * 2 * values]).astype(bf16)
+            jnp.where(position == 2 * ry, actual, result[ry * 2 * values : (ry + 1) * 2 * values]).astype(bf16)
             for ry in range(3)
         ]
         for half in range(2):
@@ -216,13 +233,23 @@
     vmem = pl.BlockSpec(memory_space=pltpu.VMEM)
     smem = pl.BlockSpec(memory_space=pltpu.SMEM)
     table = jnp.asarray(readout_table(extent).astype(BF16))
-    planes = pl.pallas_call(
+    each = 128 // cells
+    width = -(-3 * cells // 128) * 128
+    sets = nkz // GROUP
+    taps = 10 * 128 * sets
+    pitch = cells + 2 * EDGE
+    lattice = jax.ShapeDtypeStruct((sets * xs * pitch, 128), jnp.float32)
+    near, far, weights = pl.pallas_call(
         functools.partial(gather_kernel, nkz, ngx),
-        out_shape=jax.ShapeDtypeStruct((nkz, ngx, xs, 128), jnp.bfloat16),
-        in_specs=[vmem] * 3,
-        out_specs=vmem,
+        out_shape=(lattice, lattice, jax.ShapeDtypeStruct((16 * coils, taps), jnp.bfloat16)),
+        in_specs=[smem, smem, pl.BlockSpec(memory_space=pl.ANY)] + [vmem] * 6,
+        out_specs=(vmem, vmem, vmem),
         scratch_shapes=[
+            pltpu.VMEM((extent, 2 * extent), jnp.bfloat16),
+            pltpu.VMEM((nkz, ngx, xs, 128), jnp.bfloat16),
             pltpu.VMEM((ngx, xs, 128), jnp.bfloat16),
+            pltpu.VMEM((14 * coils, taps), jnp.bfloat16),
+            pltpu.SemaphoreType.DMA,
             pltpu.SemaphoreType.DMA((ngx,)),
             pltpu.SemaphoreType.DMA((ngx,)),
             pltpu.SemaphoreType.DMA((nkz, ngx)),
@@ -230,30 +257,18 @@
         ],
         compiler_params=pltpu.CompilerParams(
             collective_id=0, has_side_effects=True, vmem_limit_bytes=LIMIT),
-    )(table, kspace_lines.reshape(coils * own * 2, extent), jnp.asarray(line_order(coils, own)))
-
-    each = 128 // cells
-    width = -(-3 * cells // 128) * 128
-    sets = nkz // GROUP
-    taps = 10 * 128 * sets
-    pitch = cells + 2 * EDGE
+    )(
+        ky_start, kz_start, table, kspace_lines, jnp.asarray(line_order(coils, own)),
+        jnp.transpose(kernels, (0, 1, 3, 2, 4)), jnp.asarray(slab_order(2 * coils)),
+        jnp.asarray(weight_lanes(coils)), jnp.asarray(row_order(coils)),
+    )
     filled = pl.pallas_call(
-        functools.partial(fill_kernel, nkz),
+        functools.partial(fill_kernel, sets, xs),
         out_shape=jax.ShapeDtypeStruct((2 * xs, 2 * coils, 3 * cells), jnp.bfloat16),
-        in_specs=[smem, smem] + [vmem] * 7,
+        in_specs=[vmem] * 5,
         out_specs=vmem,
-        scratch_shapes=[
-            pltpu.VMEM((sets * xs * pitch, 128), jnp.float32),
-            pltpu.VMEM((sets * xs * pitch, 128), jnp.float32),
-            pltpu.VMEM((14 * coils, taps), jnp.bfloat16),
-            pltpu.VMEM((16 * coils, taps), jnp.bfloat16),
-        ],
         compiler_params=pltpu.CompilerParams(vmem_limit_bytes=LIMIT),
-    )(
-        ky_start, kz_start, planes, jnp.transpose(kernels, (0, 1, 3, 2, 4)),
-        jnp.tile(acquired_at, (1, 2 * each)), jnp.asarray(slab_order(2 * coils)),
-        jnp.asarray(weight_lanes(coils)), jnp.asarray(row_order(coils)), jnp.asarray(lane_order(cells, width)),
-    )
+    )(near, far, weights, acquired_at, jnp.asarray(lane_order(cells, width)))
     return filled.reshape(2, xs, coils, 2, 3 * cells)
 
 

time: 27.9 us -> 35.3 us (1.27)
  local copies, waits for them, and re-layouts: 2.99 us -> 10.7 us
  Pallas kernels: 24.6 us -> 24.2 us
    unnamed x20 -> x26, local copies, waits for them, and re-layouts: 1.91 us -> 10.7 us
    reshape x1 -> x0, local copies, waits for them, and re-layouts: 0.99 us -> none  [local(): kspace_lines.reshape(coils * own * 2, extent)]
    pallas_call x2, Pallas kernels: 24.6 us -> 24.2 us  [the longest x1 18.6 us: local(): pl.pallas_call(functools.partial(gather_kernel, nkz, ngx), out_shape=(lat...]
where the time goes in v2:
time: 35.3 us; the launch traced here: 34.9 us
  Pallas kernels  24.2 us (69%)
  local copies, waits for them, and re-layouts  10.7 us (30%)
    pallas_call x1, Pallas kernels, local(): pl.pallas_call(functools.partial(gather_kernel, nkz, ngx), out_shape=(lat...  18.6 us
    unnamed x26, local copies, waits for them, and re-layouts  10.7 us
    pallas_call x1, Pallas kernels, local(): pl.pallas_call(functools.partial(fill_kernel, sets, xs), out_shape=jax.Sh...  5.64 us

profile of v2, /device:TPU:0, one launch (start us, length us, event | category | flops | bytes accessed | tf_op | source)
XLA Modules:
  0.0 34.9 jit_solution(9013995052892115747)
XLA Ops:
  0.0 0.0 copy-start.10
  0.0 0.0 copy-start.2
  0.0 1.2 %copy-done.2 = bf16[512,1024]{1,0:T(8,128)(2,1)S(1)} copy-done((bf16[512,1024]{1,0:T(8,128)(2,1)S(1)}, bf16[512,1024]{1,0:T(8,128)(2,1)}, u32[]{:S(2)}) %copy-start.2) | copy-done | bytes 1048600
  1.2 0.0 copy-start.3
  1.2 1.0 %copy-done.3 = bf16[512,512]{1,0:T(8,128)(2,1)S(1)} copy-done((bf16[512,512]{1,0:T(8,128)(2,1)S(1)}, bf16[512,512]{1,0:T(8,128)(2,1)}, u32[]{:S(2)}) %copy-start.3) | copy-done | bytes 524312
  2.3 0.0 copy-start.5
  2.3 1.0 %copy-done.5 = bf16[2,6,16,6,32]{4,2,3,1,0:T(8,128)(2,1)S(1)} copy-done((bf16[2,6,16,6,32]{4,2,3,1,0:T(8,128)(2,1)S(1)}, bf16[2,6,16,6,32]{4,2,3,1,0:T(8,128)(2,1)}, u32[]{:S(2)}) %copy-start.5) | copy-done | bytes 73752
  3.2 0.0 copy-start.6
  3.2 0.9 %copy-done.6 = bf16[16,1,4,2,512]{4,3,2,1,0:T(2,128)(2,1)S(1)} copy-done((bf16[16,1,4,2,512]{4,3,2,1,0:T(2,128)(2,1)S(1)}, bf16[16,1,4,2,512]{4,3,2,1,0:T(2,128)(2,1)}, u32[]{:S(2)}) %copy-start.6) | copy-done | bytes 131096
  4.2 0.0 copy-start.7
  4.2 0.9 %copy-done.7 = bf16[256,224]{1,0:T(8,128)(2,1)S(1)} copy-done((bf16[256,224]{1,0:T(8,128)(2,1)S(1)}, bf16[256,224]{1,0:T(8,128)(2,1)}, u32[]{:S(2)}) %copy-start.7) | copy-done | bytes 114712
  5.1 0.0 copy-start.8
  5.1 0.8 %copy-done.8 = bf16[2,32,512]{2,1,0:T(8,128)(2,1)S(1)} copy-done((bf16[2,32,512]{2,1,0:T(8,128)(2,1)S(1)}, bf16[2,32,512]{2,1,0:T(8,128)(2,1)}, u32[]{:S(2)}) %copy-start.8) | copy-done | bytes 65560
  5.9 0.0 copy-start.9
  5.9 0.8 %copy-done.9 = bf16[256,128]{1,0:T(8,128)(2,1)S(1)} copy-done((bf16[256,128]{1,0:T(8,128)(2,1)S(1)}, bf16[256,128]{1,0:T(8,128)(2,1)}, u32[]{:S(2)}) %copy-start.9) | copy-done | bytes 65560
  6.7 0.0 copy-start.11
  6.7 0.7 %copy-done.11 = s32[6]{0:T(128)S(1)} copy-done((s32[6]{0:T(128)S(1)}, s32[6]{0:T(128)}, u32[]{:S(2)}) %copy-start.11) | copy-done | bytes 48
  7.4 0.0 copy-start.12
  7.4 0.7 %copy-done.12 = s32[6]{0:T(128)S(1)} copy-done((s32[6]{0:T(128)S(1)}, s32[6]{0:T(128)}, u32[]{:S(2)}) %copy-start.12) | copy-done | bytes 48
  8.0 0.0 copy-start.4
  8.0 18.6 %shard_map.109 = (f32[2560,128]{1,0:T(8,128)}, f32[2560,128]{1,0:T(8,128)}, bf16[256,1280]{1,0:T(8,128)(2,1)S(1)}) custom-call(s32[6]{0:T(128)S(1)} %copy-done.11, s32[6]{0:T(128)S(1)} %copy-done.12, bf16[512,1024]{1,0:T(8,128)(2,1)S(1)} %copy-done.2, bf16[16,1,4,2,512]{4,3,2,1,0:T(2,128)(2,1)S(1)} %copy-done.6, bf16[256,128]{1,0:T(8,128)(2,1)S(1)} %copy-done.9, ...), custom_call_target="tpu_custom_call" | custom-call | tf_op jit(solution)/shard_map/pallas_call | solution.py:242
  26.6 0.0 copy-done.10
  26.6 0.0 copy-done.4
  26.6 0.0 copy-start
  26.6 1.3 %copy-done = f32[2560,128]{1,0:T(8,128)S(1)} copy-done((f32[2560,128]{1,0:T(8,128)S(1)}, f32[2560,128]{1,0:T(8,128)}, u32[]{:S(2)}) %copy-start) | copy-done | bytes 1310744
  28.0 0.0 copy-start.1
  28.0 1.3 %copy-done.1 = f32[2560,128]{1,0:T(8,128)S(1)} copy-done((f32[2560,128]{1,0:T(8,128)S(1)}, f32[2560,128]{1,0:T(8,128)}, u32[]{:S(2)}) %copy-start.1) | copy-done | bytes 1310744
  29.3 5.6 %shard_map.110 = bf16[128,32,96]{2,1,0:T(8,128)(2,1)} custom-call(f32[2560,128]{1,0:T(8,128)S(1)} %copy-done, f32[2560,128]{1,0:T(8,128)S(1)} %copy-done.1, bf16[256,1280]{1,0:T(8,128)(2,1)S(1)} %get-tuple-element.10.weights, s32[1,32]{1,0:T(1,128)S(1)} %copy-done.10, bf16[384,512]{1,0:T(8,128)(2,1)S(1)} %copy-done.4), custom_call_target="tpu_custom_call" | custom-call | tf_op jit(solution)/shard_map/pallas_call | solution.py:265
Async XLA Ops:
  0.0 26.6 %copy-start.10 = (s32[1,32]{1,0:T(1,128)S(1)}, s32[1,32]{1,0:T(1,128)}, u32[]{:S(2)}) copy-start(s32[1,32]{1,0:T(1,128)} %acquired.1) | copy-start | bytes 388
  0.0 1.2 %copy-start.2 = (bf16[512,1024]{1,0:T(8,128)(2,1)S(1)}, bf16[512,1024]{1,0:T(8,128)(2,1)}, u32[]{:S(2)}) copy-start(bf16[512,1024]{1,0:T(8,128)(2,1)} %constant.12.clone.table_hbm) | copy-start | bytes 3145732
  1.2 1.0 %copy-start.3 = (bf16[512,512]{1,0:T(8,128)(2,1)S(1)}, bf16[512,512]{1,0:T(8,128)(2,1)}, u32[]{:S(2)}) copy-start(bf16[512,512]{1,0:T(8,128)(2,1)} %constant.14.clone.to_slabs) | copy-start | bytes 1572868
  2.3 1.0 %copy-start.5 = (bf16[2,6,16,6,32]{4,2,3,1,0:T(8,128)(2,1)S(1)}, bf16[2,6,16,6,32]{4,2,3,1,0:T(8,128)(2,1)}, u32[]{:S(2)}) copy-start(bf16[2,6,16,6,32]{4,2,3,1,0:T(8,128)(2,1)} %param.15) | copy-start | bytes 221188
  3.2 0.9 %copy-start.6 = (bf16[16,1,4,2,512]{4,3,2,1,0:T(2,128)(2,1)S(1)}, bf16[16,1,4,2,512]{4,3,2,1,0:T(2,128)(2,1)}, u32[]{:S(2)}) copy-start(bf16[16,1,4,2,512]{4,3,2,1,0:T(2,128)(2,1)} %lines.1) | copy-start | bytes 393220
  4.2 0.9 %copy-start.7 = (bf16[256,224]{1,0:T(8,128)(2,1)S(1)}, bf16[256,224]{1,0:T(8,128)(2,1)}, u32[]{:S(2)}) copy-start(bf16[256,224]{1,0:T(8,128)(2,1)} %constant.16.clone.to_rows) | copy-start | bytes 344068
  5.1 0.8 %copy-start.8 = (bf16[2,32,512]{2,1,0:T(8,128)(2,1)S(1)}, bf16[2,32,512]{2,1,0:T(8,128)(2,1)}, u32[]{:S(2)}) copy-start(bf16[2,32,512]{2,1,0:T(8,128)(2,1)} %constant.15.clone.to_lanes) | copy-start | bytes 196612
  5.9 0.8 %copy-start.9 = (bf16[256,128]{1,0:T(8,128)(2,1)S(1)}, bf16[256,128]{1,0:T(8,128)(2,1)}, u32[]{:S(2)}) copy-start(bf16[256,128]{1,0:T(8,128)(2,1)} %constant.13.clone.order) | copy-start | bytes 196612
  6.7 0.7 %copy-start.11 = (s32[6]{0:T(128)S(1)}, s32[6]{0:T(128)}, u32[]{:S(2)}) copy-start(s32[6]{0:T(128)} %ky_start.1) | copy-start | bytes 76
  7.4 0.7 %copy-start.12 = (s32[6]{0:T(128)S(1)}, s32[6]{0:T(128)}, u32[]{:S(2)}) copy-start(s32[6]{0:T(128)} %kz_start.1) | copy-start | bytes 76
  8.0 18.6 %copy-start.4 = (bf16[384,512]{1,0:T(8,128)(2,1)S(1)}, bf16[384,512]{1,0:T(8,128)(2,1)}, u32[]{:S(2)}) copy-start(bf16[384,512]{1,0:T(8,128)(2,1)} %constant.17.clone.to_ky) | copy-start | bytes 1179652
  26.6 1.3 %copy-start = (f32[2560,128]{1,0:T(8,128)S(1)}, f32[2560,128]{1,0:T(8,128)}, u32[]{:S(2)}) copy-start(f32[2560,128]{1,0:T(8,128)} %get-tuple-element.8.near) | copy-start | bytes 3932164
  28.0 1.3 %copy-start.1 = (f32[2560,128]{1,0:T(8,128)S(1)}, f32[2560,128]{1,0:T(8,128)}, u32[]{:S(2)}) copy-start(f32[2560,128]{1,0:T(8,128)} %get-tuple-element.9.far) | copy-start | bytes 3932164

commit v3 on v2

--- a/solution.py
+++ b/solution.py
@@ -14,7 +14,7 @@
 MESH = pl.DeviceIdType.MESH
 GROUP = 4
 EDGE = 4
-LIMIT = 50 * 1024 * 1024
+LIMIT = 60 * 1024 * 1024
 
 
 def readout_table(extent):
@@ -80,16 +80,19 @@
     return lax.dot_general(left, right, (((1,), (1,)), ((), ())), preferred_element_type=jnp.float32)
 
 
-def gather_kernel(nkz, ngx, ky_start, kz_start, table_hbm, lines, order, parts, to_slabs, to_lanes, to_rows,
-                  near, far, weights, table, planes, spectra, natural, load, send_x, recv_x, send_z, recv_z):
+def kernel(nkz, ngx, *refs):
+    sources, out, held = refs[:11], refs[11], refs[12:23]
+    lines, order, table, parts, to_lanes, ky_start, kz_start, to_rows, to_slabs, acquired, to_ky = held
+    near, far, weights, planes, spectra, natural, chosen, load, send_x, recv_x, send_z, recv_z = refs[23:]
     b, g = lax.axis_index("kz"), lax.axis_index("gx")
     barrier = pltpu.get_barrier_semaphore()
     for k in range(1, ngx):
         pl.semaphore_signal(barrier, inc=1, device_id=(b, lax.rem(g + k, ngx)), device_id_type=MESH)
     for j in range(1, nkz):
         pl.semaphore_signal(barrier, inc=1, device_id=(lax.rem(b + j, nkz), g), device_id_type=MESH)
-    loading = pltpu.make_async_copy(table_hbm, table, load)
-    loading.start()
+    loading = [pltpu.make_async_copy(*pair, load.at[n]) for n, pair in enumerate(zip(sources, held))]
+    for copy in loading:
+        copy.start()
 
     f32, bf16 = jnp.float32, jnp.bfloat16
     sets = nkz // GROUP
@@ -100,16 +103,18 @@
     xs = spectra.shape[1]
 
     count = values * GROUP
+    for copy in loading[:2]:
+        copy.wait()
     both = jnp.dot(order[...], lines[...].reshape(count, table.shape[0]), preferred_element_type=f32).astype(bf16)
     right = jnp.concatenate([both[:count], both[count:]], axis=1)
+    for copy in loading[2:]:
+        copy.wait()
+    spectra[...] = nt(table[...], right).astype(bf16).reshape(spectra.shape)
+    planes[b, g] = spectra[g]
     terms = (
         jnp.dot(parts[0].reshape(36 * coils, values), to_lanes[0], preferred_element_type=f32)
         + jnp.dot(parts[1].reshape(36 * coils, values), to_lanes[1], preferred_element_type=f32)
     )
-    loading.wait()
-    spectra[...] = nt(table[...], right).astype(bf16).reshape(spectra.shape)
-    planes[b, g] = spectra[g]
-
     pl.semaphore_wait(barrier, ngx + nkz - 2)
     along_x, along_z = {}, {}
 
@@ -189,15 +194,7 @@
                 base = part * xs * pitch + EDGE
                 near[pl.ds(base + source * GROUP + n, xs, stride=pitch), :] = piece
                 far[pl.ds(base + cells - 1 - n - source * GROUP, xs, stride=pitch), :] = piece
-    for copy in list(along_x.values()) + list(along_z.values()):
-        copy.wait_send()
-
-
-def fill_kernel(sets, xs, near, far, weights, acquired, to_ky, out):
-    cells = acquired.shape[1]
-    values = weights.shape[0] // 8
-    pitch = cells + 2 * EDGE
-    f32, bf16 = jnp.float32, jnp.bfloat16
+
     each = 128 // cells
     width = to_ky.shape[1] // each
     step = 2 * each
@@ -212,17 +209,23 @@
                     pieces.append(jnp.concatenate([buffer[r : r + cells, :] for r in rows], axis=0).astype(bf16))
         result = nt(weights[...], jnp.concatenate(pieces, axis=1))
         actual = result[6 * values :]
-        chosen = [
-            jnp.where(position == 2 * ry, actual, result[ry * 2 * values : (ry + 1) * 2 * values]).astype(bf16)
-            for ry in range(3)
-        ]
-        for half in range(2):
-            line = jnp.concatenate([c[:, half * 128 : (half + 1) * 128] for c in chosen], axis=1)
-            spread = jnp.dot(line, to_ky[...], preferred_element_type=f32).astype(bf16)
+        for ry in range(3):
+            estimate = result[ry * 2 * values : (ry + 1) * 2 * values]
+            picked = jnp.where(position == 2 * ry, actual, estimate).astype(bf16)
+            for half in range(2):
+                at = (start // each + half) * 2 * values
+                chosen[at : at + 2 * values, ry * 128 : (ry + 1) * 128] = picked[:, half * 128 : (half + 1) * 128]
+    batch = chosen.shape[0] // 2
+    for at in range(0, 2 * batch, batch):
+        spread = jnp.dot(chosen[at : at + batch, :], to_ky[...], preferred_element_type=f32).astype(bf16)
+        for row in range(0, batch, 2 * values):
             for n in range(each):
-                x = start + half * each + n
+                x = (at + row) // (2 * values) * each + n
                 for s in range(2):
-                    out[s * xs + x] = spread[s * values : (s + 1) * values, n * width : n * width + 3 * cells]
+                    first = row + s * values
+                    out[s * xs + x] = spread[first : first + values, n * width : n * width + 3 * cells]
+    for copy in list(along_x.values()) + list(along_z.values()):
+        copy.wait_send()
 
 
 def local(kspace_lines, acquired_at, ky_start, kz_start, kernels):
@@ -230,26 +233,39 @@
     coils, _, own, _, extent = kspace_lines.shape
     xs, cells = extent // ngx, ngx * own
     assert own == GROUP and nkz % GROUP == 0 and 2 * coils * GROUP == 128 and 128 % cells == 0
-    vmem = pl.BlockSpec(memory_space=pltpu.VMEM)
-    smem = pl.BlockSpec(memory_space=pltpu.SMEM)
-    table = jnp.asarray(readout_table(extent).astype(BF16))
     each = 128 // cells
     width = -(-3 * cells // 128) * 128
     sets = nkz // GROUP
     taps = 10 * 128 * sets
-    pitch = cells + 2 * EDGE
-    lattice = jax.ShapeDtypeStruct((sets * xs * pitch, 128), jnp.float32)
-    near, far, weights = pl.pallas_call(
-        functools.partial(gather_kernel, nkz, ngx),
-        out_shape=(lattice, lattice, jax.ShapeDtypeStruct((16 * coils, taps), jnp.bfloat16)),
-        in_specs=[smem, smem, pl.BlockSpec(memory_space=pl.ANY)] + [vmem] * 6,
-        out_specs=(vmem, vmem, vmem),
-        scratch_shapes=[
-            pltpu.VMEM((extent, 2 * extent), jnp.bfloat16),
+    lattice = pltpu.VMEM((sets * xs * (cells + 2 * EDGE), 128), jnp.float32)
+    operands = [
+        kspace_lines,
+        jnp.asarray(line_order(coils, own)),
+        jnp.asarray(readout_table(extent).astype(BF16)),
+        jnp.transpose(kernels, (0, 1, 3, 2, 4)),
+        jnp.asarray(weight_lanes(coils)),
+        ky_start,
+        kz_start,
+        jnp.asarray(row_order(coils)),
+        jnp.asarray(slab_order(2 * coils)),
+        acquired_at,
+        jnp.asarray(lane_order(cells, width)),
+    ]
+    held = [pltpu.SMEM(o.shape, o.dtype) if o.ndim == 1 else pltpu.VMEM(o.shape, o.dtype) for o in operands]
+    filled = pl.pallas_call(
+        functools.partial(kernel, nkz, ngx),
+        out_shape=jax.ShapeDtypeStruct((2 * xs, 2 * coils, 3 * cells), jnp.bfloat16),
+        in_specs=[pl.BlockSpec(memory_space=pltpu.HBM)] * len(operands),
+        out_specs=pl.BlockSpec(memory_space=pltpu.VMEM),
+        scratch_shapes=held + [
+            lattice,
+            lattice,
+            pltpu.VMEM((16 * coils, taps), jnp.bfloat16),
             pltpu.VMEM((nkz, ngx, xs, 128), jnp.bfloat16),
             pltpu.VMEM((ngx, xs, 128), jnp.bfloat16),
             pltpu.VMEM((14 * coils, taps), jnp.bfloat16),
-            pltpu.SemaphoreType.DMA,
+            pltpu.VMEM((xs // each * 4 * coils, 3 * 128), jnp.bfloat16),
+            pltpu.SemaphoreType.DMA((len(operands),)),
             pltpu.SemaphoreType.DMA((ngx,)),
             pltpu.SemaphoreType.DMA((ngx,)),
             pltpu.SemaphoreType.DMA((nkz, ngx)),
@@ -257,18 +273,7 @@
         ],
         compiler_params=pltpu.CompilerParams(
             collective_id=0, has_side_effects=True, vmem_limit_bytes=LIMIT),
-    )(
-        ky_start, kz_start, table, kspace_lines, jnp.asarray(line_order(coils, own)),
-        jnp.transpose(kernels, (0, 1, 3, 2, 4)), jnp.asarray(slab_order(2 * coils)),
-        jnp.asarray(weight_lanes(coils)), jnp.asarray(row_order(coils)),
-    )
-    filled = pl.pallas_call(
-        functools.partial(fill_kernel, sets, xs),
-        out_shape=jax.ShapeDtypeStruct((2 * xs, 2 * coils, 3 * cells), jnp.bfloat16),
-        in_specs=[vmem] * 5,
-        out_specs=vmem,
-        compiler_params=pltpu.CompilerParams(vmem_limit_bytes=LIMIT),
-    )(near, far, weights, acquired_at, jnp.asarray(lane_order(cells, width)))
+    )(*operands)
     return filled.reshape(2, xs, coils, 2, 3 * cells)
 
 

time: 35.3 us -> 23.9 us (0.68)
  local copies, waits for them, and re-layouts: 10.7 us -> 2.92 us
  Pallas kernels: 24.2 us -> 20.8 us
    unnamed x26 -> x1, local copies, waits for them, and re-layouts: 10.7 us -> 2.92 us
    pallas_call x2 -> x1, Pallas kernels: 24.2 us -> 20.8 us  [local(): pl.pallas_call(functools.partial(kernel, nkz, ngx), out_shape=jax.ShapeDt...]
where the time goes in v3:
time: 23.9 us; the launch traced here: 23.7 us
  Pallas kernels  20.8 us (87%)
  local copies, waits for them, and re-layouts  2.92 us (12%)
    pallas_call x1, Pallas kernels, local(): pl.pallas_call(functools.partial(kernel, nkz, ngx), out_shape=jax.ShapeDt...  20.8 us
    unnamed x1, local copies, waits for them, and re-layouts  2.92 us

profile of v3, /device:TPU:0, one launch (start us, length us, event | category | flops | bytes accessed | tf_op | source)
XLA Modules:
  0.0 23.7 jit_solution(1863853118371826817)
XLA Ops:
  0.0 20.8 %shard_map.109 = bf16[128,32,96]{2,1,0:T(8,128)(2,1)} custom-call(bf16[16,1,4,2,512]{4,3,2,1,0:T(2,128)(2,1)} %refs_0_.1, bf16[256,128]{1,0:T(8,128)(2,1)} %constant.12.clone.refs_1_, bf16[512,1024]{1,0:T(8,128)(2,1)} %constant.13.clone.refs_2_, bf16[2,6,6,16,32]{4,3,2,1,0:T(8,128)(2,1)} %bitcast.3, bf16[2,32,512]{2,1,0:T(8,128)(2,1)} %constant.14.clone.refs_4_, ...), custom_call_target="tpu_custom_call" | custom-call | tf_op jit(solution)/shard_map/pallas_call | solution.py:255
  20.8 2.9 %copy.13 = bf16[2,64,16,2,96]{4,3,2,1,0:T(2,128)(2,1)} copy(bf16[2,64,16,2,96]{4,3,2,1,0:T(2,128)(2,1)} %bitcast.2) | data formatting | bytes 1572864

commit v4 on v3

--- a/solution.py
+++ b/solution.py
@@ -83,7 +83,7 @@
 def kernel(nkz, ngx, *refs):
     sources, out, held = refs[:11], refs[11], refs[12:23]
     lines, order, table, parts, to_lanes, ky_start, kz_start, to_rows, to_slabs, acquired, to_ky = held
-    near, far, weights, planes, spectra, natural, chosen, load, send_x, recv_x, send_z, recv_z = refs[23:]
+    near, far, weights, planes, spectra, natural, chosen, staged, load, unload, send_x, recv_x, send_z, recv_z = refs[23:]
     b, g = lax.axis_index("kz"), lax.axis_index("gx")
     barrier = pltpu.get_barrier_semaphore()
     for k in range(1, ngx):
@@ -107,14 +107,10 @@
         copy.wait()
     both = jnp.dot(order[...], lines[...].reshape(count, table.shape[0]), preferred_element_type=f32).astype(bf16)
     right = jnp.concatenate([both[:count], both[count:]], axis=1)
-    for copy in loading[2:]:
-        copy.wait()
+    loading[2].wait()
     spectra[...] = nt(table[...], right).astype(bf16).reshape(spectra.shape)
     planes[b, g] = spectra[g]
-    terms = (
-        jnp.dot(parts[0].reshape(36 * coils, values), to_lanes[0], preferred_element_type=f32)
-        + jnp.dot(parts[1].reshape(36 * coils, values), to_lanes[1], preferred_element_type=f32)
-    )
+
     pl.semaphore_wait(barrier, ngx + nkz - 2)
     along_x, along_z = {}, {}
 
@@ -133,6 +129,13 @@
             recv_sem=recv_x.at[k], device_id=(b, to), device_id_type=MESH)
         along_x[k].start()
     forward(0)
+
+    for copy in loading[3:]:
+        copy.wait()
+    terms = (
+        jnp.dot(parts[0].reshape(36 * coils, values), to_lanes[0], preferred_element_type=f32)
+        + jnp.dot(parts[1].reshape(36 * coils, values), to_lanes[1], preferred_element_type=f32)
+    )
 
     lane = lax.broadcasted_iota(jnp.int32, (coils, 128), 1)
     slab = lane // values
@@ -216,6 +219,7 @@
                 at = (start // each + half) * 2 * values
                 chosen[at : at + 2 * values, ry * 128 : (ry + 1) * 128] = picked[:, half * 128 : (half + 1) * 128]
     batch = chosen.shape[0] // 2
+    leaving = []
     for at in range(0, 2 * batch, batch):
         spread = jnp.dot(chosen[at : at + batch, :], to_ky[...], preferred_element_type=f32).astype(bf16)
         for row in range(0, batch, 2 * values):
@@ -223,9 +227,29 @@
                 x = (at + row) // (2 * values) * each + n
                 for s in range(2):
                     first = row + s * values
-                    out[s * xs + x] = spread[first : first + values, n * width : n * width + 3 * cells]
+                    staged[s * xs + x] = spread[first : first + values, n * width : n * width + 3 * cells]
+        half = xs * batch // chosen.shape[0]
+        for s in range(2):
+            part = pl.ds(s * xs + at // batch * half, half)
+            leaving.append(pltpu.make_async_copy(staged.at[part], out.at[part], unload.at[len(leaving)]))
+            leaving[-1].start()
     for copy in list(along_x.values()) + list(along_z.values()):
         copy.wait_send()
+    for copy in leaving:
+        copy.wait()
+
+
+def copy_kernel(source, target, sems):
+    count = sems.shape[0]
+    size = source.shape[0] // count
+    copies = [
+        pltpu.make_async_copy(source.at[pl.ds(n * size, size)], target.at[pl.ds(n * size, size)], sems.at[n])
+        for n in range(count)
+    ]
+    for copy in copies:
+        copy.start()
+    for copy in copies:
+        copy.wait()
 
 
 def local(kspace_lines, acquired_at, ky_start, kz_start, kernels):
@@ -256,7 +280,7 @@
         functools.partial(kernel, nkz, ngx),
         out_shape=jax.ShapeDtypeStruct((2 * xs, 2 * coils, 3 * cells), jnp.bfloat16),
         in_specs=[pl.BlockSpec(memory_space=pltpu.HBM)] * len(operands),
-        out_specs=pl.BlockSpec(memory_space=pltpu.VMEM),
+        out_specs=pl.BlockSpec(memory_space=pltpu.HBM),
         scratch_shapes=held + [
             lattice,
             lattice,
@@ -265,7 +289,9 @@
             pltpu.VMEM((ngx, xs, 128), jnp.bfloat16),
             pltpu.VMEM((14 * coils, taps), jnp.bfloat16),
             pltpu.VMEM((xs // each * 4 * coils, 3 * 128), jnp.bfloat16),
+            pltpu.VMEM((2 * xs, 2 * coils, 3 * cells), jnp.bfloat16),
             pltpu.SemaphoreType.DMA((len(operands),)),
+            pltpu.SemaphoreType.DMA((4,)),
             pltpu.SemaphoreType.DMA((ngx,)),
             pltpu.SemaphoreType.DMA((ngx,)),
             pltpu.SemaphoreType.DMA((nkz, ngx)),
@@ -274,6 +300,14 @@
         compiler_params=pltpu.CompilerParams(
             collective_id=0, has_side_effects=True, vmem_limit_bytes=LIMIT),
     )(*operands)
+    filled = pl.pallas_call(
+        copy_kernel,
+        out_shape=jax.ShapeDtypeStruct(filled.shape, filled.dtype),
+        in_specs=[pl.BlockSpec(memory_space=pltpu.HBM)],
+        out_specs=pl.BlockSpec(memory_space=pltpu.HBM),
+        scratch_shapes=[pltpu.SemaphoreType.DMA((8,))],
+        compiler_params=pltpu.CompilerParams(vmem_limit_bytes=LIMIT),
+    )(filled)
     return filled.reshape(2, xs, coils, 2, 3 * cells)
 
 

time: 23.9 us -> 53.2 us (2.23)
  Pallas kernels: 20.8 us -> 53.1 us
  local copies, waits for them, and re-layouts: 2.92 us -> 0 us
    pallas_call x0 -> x1, Pallas kernels: none -> 32.9 us  [local(): pl.pallas_call(copy_kernel, out_shape=jax.ShapeDtypeStruct(filled.shape,...]
    unnamed x1 -> x0, local copies, waits for them, and re-layouts: 2.92 us -> none
    pallas_call x1, Pallas kernels: 20.8 us -> 20.1 us  [local(): pl.pallas_call(functools.partial(kernel, nkz, ngx), out_shape=jax.ShapeDt...]
where the time goes in v4:
time: 53.2 us; the launch traced here: 53.1 us
  Pallas kernels  53.1 us (100%)
    pallas_call x1, Pallas kernels, local(): pl.pallas_call(copy_kernel, out_shape=jax.ShapeDtypeStruct(filled.shape,...  32.9 us
    pallas_call x1, Pallas kernels, local(): pl.pallas_call(functools.partial(kernel, nkz, ngx), out_shape=jax.ShapeDt...  20.1 us

profile of v4, /device:TPU:0, one launch (start us, length us, event | category | flops | bytes accessed | tf_op | source)
XLA Modules:
  0.0 53.1 jit_solution(10812243183634578955)
XLA Ops:
  0.0 20.1 %shard_map.109.source = bf16[128,32,96]{2,1,0:T(8,128)(2,1)} custom-call(bf16[16,1,4,2,512]{4,3,2,1,0:T(2,128)(2,1)} %refs_0_.1, bf16[256,128]{1,0:T(8,128)(2,1)} %constant.12.clone.refs_1_, bf16[512,1024]{1,0:T(8,128)(2,1)} %constant.13.clone.refs_2_, bf16[2,6,6,16,32]{4,3,2,1,0:T(8,128)(2,1)} %bitcast.2, bf16[2,32,512]{2,1,0:T(8,128)(2,1)} %constant.14.clone.refs_4_, ...), custom_call_target="tpu_custom_call" | custom-call | tf_op jit(solution)/shard_map/pallas_call | solution.py:279
  20.1 32.9 %shard_map.110 = bf16[128,32,96]{2,1,0:T(8,128)(2,1)} custom-call(bf16[128,32,96]{2,1,0:T(8,128)(2,1)} %shard_map.109.source), custom_call_target="tpu_custom_call" | custom-call | tf_op jit(solution)/shard_map/pallas_call | solution.py:303

commit v5 on v4

--- a/solution.py
+++ b/solution.py
@@ -239,17 +239,23 @@
         copy.wait()
 
 
-def copy_kernel(source, target, sems):
-    count = sems.shape[0]
+def copy_kernel(source, target, held, entering, leaving):
+    count = entering.shape[0]
     size = source.shape[0] // count
-    copies = [
-        pltpu.make_async_copy(source.at[pl.ds(n * size, size)], target.at[pl.ds(n * size, size)], sems.at[n])
-        for n in range(count)
-    ]
-    for copy in copies:
-        copy.start()
-    for copy in copies:
-        copy.wait()
+    pairs = []
+    for n in range(count):
+        part = pl.ds(n * size, size)
+        pairs.append((
+            pltpu.make_async_copy(source.at[part], held.at[part], entering.at[n]),
+            pltpu.make_async_copy(held.at[part], target.at[part], leaving.at[n]),
+        ))
+    for first, _ in pairs:
+        first.start()
+    for first, second in pairs:
+        first.wait()
+        second.start()
+    for _, second in pairs:
+        second.wait()
 
 
 def local(kspace_lines, acquired_at, ky_start, kz_start, kernels):
@@ -305,7 +311,11 @@
         out_shape=jax.ShapeDtypeStruct(filled.shape, filled.dtype),
         in_specs=[pl.BlockSpec(memory_space=pltpu.HBM)],
         out_specs=pl.BlockSpec(memory_space=pltpu.HBM),
-        scratch_shapes=[pltpu.SemaphoreType.DMA((8,))],
+        scratch_shapes=[
+            pltpu.VMEM(filled.shape, filled.dtype),
+            pltpu.SemaphoreType.DMA((8,)),
+            pltpu.SemaphoreType.DMA((8,)),
+        ],
         compiler_params=pltpu.CompilerParams(vmem_limit_bytes=LIMIT),
     )(filled)
     return filled.reshape(2, xs, coils, 2, 3 * cells)

time: 53.2 us -> 22.4 us (0.42)
  Pallas kernels: 53.1 us -> 22.2 us
    pallas_call x1, Pallas kernels: 32.9 us -> 2.09 us  [local(): pl.pallas_call(copy_kernel, out_shape=jax.ShapeDtypeStruct(filled.shape,...]
where the time goes in v5:
time: 22.4 us; the launch traced here: 22.2 us
  Pallas kernels  22.2 us (99%)
    pallas_call x1, Pallas kernels, local(): pl.pallas_call(functools.partial(kernel, nkz, ngx), out_shape=jax.ShapeDt...  20.1 us
    pallas_call x1, Pallas kernels, local(): pl.pallas_call(copy_kernel, out_shape=jax.ShapeDtypeStruct(filled.shape,...  2.09 us

profile of v5, /device:TPU:0, one launch (start us, length us, event | category | flops | bytes accessed | tf_op | source)
XLA Modules:
  0.0 22.2 jit_solution(15235194855225117464)
XLA Ops:
  0.0 20.1 %shard_map.109.source = bf16[128,32,96]{2,1,0:T(8,128)(2,1)} custom-call(bf16[16,1,4,2,512]{4,3,2,1,0:T(2,128)(2,1)} %refs_0_.1, bf16[256,128]{1,0:T(8,128)(2,1)} %constant.12.clone.refs_1_, bf16[512,1024]{1,0:T(8,128)(2,1)} %constant.13.clone.refs_2_, bf16[2,6,6,16,32]{4,3,2,1,0:T(8,128)(2,1)} %bitcast.2, bf16[2,32,512]{2,1,0:T(8,128)(2,1)} %constant.14.clone.refs_4_, ...), custom_call_target="tpu_custom_call" | custom-call | tf_op jit(solution)/shard_map/pallas_call | solution.py:285
  20.1 2.1 %shard_map.110 = bf16[128,32,96]{2,1,0:T(8,128)(2,1)} custom-call(bf16[128,32,96]{2,1,0:T(8,128)(2,1)} %shard_map.109.source), custom_call_target="tpu_custom_call" | custom-call | tf_op jit(solution)/shard_map/pallas_call | solution.py:309

commit v6 on v5

--- a/solution.py
+++ b/solution.py
@@ -100,7 +100,10 @@
     values = 2 * coils
     cells = ngx * GROUP
     pitch = cells + 2 * EDGE
-    xs = spectra.shape[1]
+    _, halves, hx, _ = spectra.shape
+    xs = halves * hx
+    pairs = ngx // 2
+    chip, core = g // 2, lax.rem(g, 2)
 
     count = values * GROUP
     for copy in loading[:2]:
@@ -109,27 +112,29 @@
     right = jnp.concatenate([both[:count], both[count:]], axis=1)
     loading[2].wait()
     spectra[...] = nt(table[...], right).astype(bf16).reshape(spectra.shape)
-    planes[b, g] = spectra[g]
+    for h in range(halves):
+        planes[b, h, g] = spectra[g, h]
 
     pl.semaphore_wait(barrier, ngx + nkz - 2)
     along_x, along_z = {}, {}
 
-    def forward(k):
-        source = lax.rem(g + ngx - k, ngx)
+    def forward(h, m):
+        block = planes.at[b, h, pl.ds(2 * lax.rem(chip + pairs - m, pairs), 2)]
         for j in range(1, nkz):
-            along_z[j, k] = pltpu.make_async_remote_copy(
-                src_ref=planes.at[b, source], dst_ref=planes.at[b, source], send_sem=send_z.at[j, k],
-                recv_sem=recv_z.at[j, k], device_id=(lax.rem(b + j, nkz), g), device_id_type=MESH)
-            along_z[j, k].start()
-
-    for k in range(1, ngx):
-        to = lax.rem(g + k, ngx)
-        along_x[k] = pltpu.make_async_remote_copy(
-            src_ref=spectra.at[to], dst_ref=planes.at[b, g], send_sem=send_x.at[k],
-            recv_sem=recv_x.at[k], device_id=(b, to), device_id_type=MESH)
-        along_x[k].start()
-    forward(0)
-
+            along_z[j, h, m] = pltpu.make_async_remote_copy(
+                src_ref=block, dst_ref=block, send_sem=send_z.at[j, h, m], recv_sem=recv_z.at[j, h, m],
+                device_id=(lax.rem(b + j, nkz), g), device_id_type=MESH)
+            along_z[j, h, m].start()
+
+    for h in range(halves):
+        for k in range(1, ngx):
+            to = 2 * lax.rem(chip + k // 2, pairs) + lax.rem(core + k % 2, 2)
+            along_x[h, k] = pltpu.make_async_remote_copy(
+                src_ref=spectra.at[to, h], dst_ref=planes.at[b, h, g], send_sem=send_x.at[h, k],
+                recv_sem=recv_x.at[h, k], device_id=(b, to), device_id_type=MESH)
+            along_x[h, k].start()
+    along_x[0, 1].wait_recv()
+    forward(0, 0)
     for copy in loading[3:]:
         copy.wait()
     terms = (
@@ -178,49 +183,58 @@
                 buffer[(x + 1) * pitch - EDGE : (x + 1) * pitch, :] = jnp.zeros((EDGE, 128), f32)
 
     work = [functools.partial(place, t) for t in range(6)] + [place_rest]
-    for k in range(1, ngx):
-        along_x[k].wait_recv()
-        forward(k)
-        if work:
-            work.pop(0)()
+    for h in range(halves):
+        for m in range(pairs):
+            if h or m:
+                for k in range(max(2 * m, 1), 2 * m + 2):
+                    along_x[h, k].wait_recv()
+                forward(h, m)
+            if work:
+                work.pop(0)()
+    for piece in work:
+        piece()
     weights[...] = jnp.dot(to_rows[...], natural[...], preferred_element_type=f32).astype(bf16)
 
-    for k in range(ngx):
-        for j in range(1, nkz):
-            along_z[j, k].wait_recv()
-        source = lax.rem(g + ngx - k, ngx)
+    def regroup(h):
+        for m in range(pairs):
+            for j in range(1, nkz):
+                along_z[j, h, m].wait_recv()
         for part in range(sets):
-            block = jnp.concatenate([planes[part * GROUP + n, source] for n in range(GROUP)], axis=1)
+            block = jnp.concatenate(
+                [planes[part * GROUP + n, h].reshape(ngx * hx, 128) for n in range(GROUP)], axis=1)
             turned = jnp.dot(block, to_slabs[...], preferred_element_type=f32)
-            for n in range(GROUP):
-                piece = turned[:, n * 128 : (n + 1) * 128]
-                base = part * xs * pitch + EDGE
-                near[pl.ds(base + source * GROUP + n, xs, stride=pitch), :] = piece
-                far[pl.ds(base + cells - 1 - n - source * GROUP, xs, stride=pitch), :] = piece
+            base = (part * xs + h * hx) * pitch + EDGE
+            for a in range(cells):
+                q, n = a // GROUP, a % GROUP
+                piece = turned[q * hx : (q + 1) * hx, n * 128 : (n + 1) * 128]
+                near[pl.ds(base + a, hx, stride=pitch), :] = piece
+                far[pl.ds(base + cells - 1 - a, hx, stride=pitch), :] = piece
 
     each = 128 // cells
     width = to_ky.shape[1] // each
     step = 2 * each
     odd = lax.broadcasted_iota(jnp.int32, (2 * values, 2 * 128), 0) % 2
     position = jnp.concatenate([acquired[...]] * step, axis=1) - odd
-    for start in range(0, xs, step):
-        pieces = []
-        for buffer in (near, far):
-            for d in range(-2, 3):
-                for part in range(sets):
-                    rows = [(part * xs + x) * pitch + EDGE + d for x in range(start, start + step)]
-                    pieces.append(jnp.concatenate([buffer[r : r + cells, :] for r in rows], axis=0).astype(bf16))
-        result = nt(weights[...], jnp.concatenate(pieces, axis=1))
-        actual = result[6 * values :]
-        for ry in range(3):
-            estimate = result[ry * 2 * values : (ry + 1) * 2 * values]
-            picked = jnp.where(position == 2 * ry, actual, estimate).astype(bf16)
-            for half in range(2):
-                at = (start // each + half) * 2 * values
-                chosen[at : at + 2 * values, ry * 128 : (ry + 1) * 128] = picked[:, half * 128 : (half + 1) * 128]
-    batch = chosen.shape[0] // 2
+    batch = chosen.shape[0] // halves
     leaving = []
-    for at in range(0, 2 * batch, batch):
+    for h in range(halves):
+        regroup(h)
+        for start in range(h * hx, (h + 1) * hx, step):
+            pieces = []
+            for buffer in (near, far):
+                for d in range(-2, 3):
+                    for part in range(sets):
+                        rows = [(part * xs + x) * pitch + EDGE + d for x in range(start, start + step)]
+                        pieces.append(jnp.concatenate([buffer[r : r + cells, :] for r in rows], axis=0).astype(bf16))
+            result = nt(weights[...], jnp.concatenate(pieces, axis=1))
+            actual = result[6 * values :]
+            for ry in range(3):
+                estimate = result[ry * 2 * values : (ry + 1) * 2 * values]
+                picked = jnp.where(position == 2 * ry, actual, estimate).astype(bf16)
+                for half in range(2):
+                    at = (start // each + half) * 2 * values
+                    chosen[at : at + 2 * values, ry * 128 : (ry + 1) * 128] = picked[:, half * 128 : (half + 1) * 128]
+        at = h * batch
         spread = jnp.dot(chosen[at : at + batch, :], to_ky[...], preferred_element_type=f32).astype(bf16)
         for row in range(0, batch, 2 * values):
             for n in range(each):
@@ -228,9 +242,8 @@
                 for s in range(2):
                     first = row + s * values
                     staged[s * xs + x] = spread[first : first + values, n * width : n * width + 3 * cells]
-        half = xs * batch // chosen.shape[0]
         for s in range(2):
-            part = pl.ds(s * xs + at // batch * half, half)
+            part = pl.ds(s * xs + h * hx, hx)
             leaving.append(pltpu.make_async_copy(staged.at[part], out.at[part], unload.at[len(leaving)]))
             leaving[-1].start()
     for copy in list(along_x.values()) + list(along_z.values()):
@@ -262,10 +275,12 @@
     nkz, ngx = lax.axis_size("kz"), lax.axis_size("gx")
     coils, _, own, _, extent = kspace_lines.shape
     xs, cells = extent // ngx, ngx * own
-    assert own == GROUP and nkz % GROUP == 0 and 2 * coils * GROUP == 128 and 128 % cells == 0
+    assert own == GROUP and ngx % 2 == 0 and nkz % GROUP == 0 and 2 * coils * GROUP == 128 and 128 % cells == 0
     each = 128 // cells
     width = -(-3 * cells // 128) * 128
     sets = nkz // GROUP
+    halves = 2 if xs % 32 == 0 else 1
+    hx = xs // halves
     taps = 10 * 128 * sets
     lattice = pltpu.VMEM((sets * xs * (cells + 2 * EDGE), 128), jnp.float32)
     operands = [
@@ -291,17 +306,17 @@
             lattice,
             lattice,
             pltpu.VMEM((16 * coils, taps), jnp.bfloat16),
-            pltpu.VMEM((nkz, ngx, xs, 128), jnp.bfloat16),
-            pltpu.VMEM((ngx, xs, 128), jnp.bfloat16),
+            pltpu.VMEM((nkz, halves, ngx, hx, 128), jnp.bfloat16),
+            pltpu.VMEM((ngx, halves, hx, 128), jnp.bfloat16),
             pltpu.VMEM((14 * coils, taps), jnp.bfloat16),
             pltpu.VMEM((xs // each * 4 * coils, 3 * 128), jnp.bfloat16),
             pltpu.VMEM((2 * xs, 2 * coils, 3 * cells), jnp.bfloat16),
             pltpu.SemaphoreType.DMA((len(operands),)),
-            pltpu.SemaphoreType.DMA((4,)),
-            pltpu.SemaphoreType.DMA((ngx,)),
-            pltpu.SemaphoreType.DMA((ngx,)),
-            pltpu.SemaphoreType.DMA((nkz, ngx)),
-            pltpu.SemaphoreType.DMA((nkz, ngx)),
+            pltpu.SemaphoreType.DMA((2 * halves,)),
+            pltpu.SemaphoreType.DMA((halves, ngx)),
+            pltpu.SemaphoreType.DMA((halves, ngx)),
+            pltpu.SemaphoreType.DMA((nkz, halves, ngx // 2)),
+            pltpu.SemaphoreType.DMA((nkz, halves, ngx // 2)),
         ],
         compiler_params=pltpu.CompilerParams(
             collective_id=0, has_side_effects=True, vmem_limit_bytes=LIMIT),

time: 22.4 us -> 22.6 us (level)
  no operation moved by 1% of the time
where the time goes in v6:
time: 22.6 us; the launch traced here: 22.4 us
  Pallas kernels  22.4 us (99%)
    pallas_call x1, Pallas kernels, local(): pl.pallas_call(functools.partial(kernel, nkz, ngx), out_shape=jax.ShapeDt...  20.4 us
    pallas_call x1, Pallas kernels, local(): pl.pallas_call(copy_kernel, out_shape=jax.ShapeDtypeStruct(filled.shape,...  2.09 us

profile of v6, /device:TPU:0, one launch (start us, length us, event | category | flops | bytes accessed | tf_op | source)
XLA Modules:
  0.0 22.4 jit_solution(15270181459139301315)
XLA Ops:
  0.0 20.4 %shard_map.109.source = bf16[128,32,96]{2,1,0:T(8,128)(2,1)} custom-call(bf16[16,1,4,2,512]{4,3,2,1,0:T(2,128)(2,1)} %refs_0_.1, bf16[256,128]{1,0:T(8,128)(2,1)} %constant.12.clone.refs_1_, bf16[512,1024]{1,0:T(8,128)(2,1)} %constant.13.clone.refs_2_, bf16[2,6,6,16,32]{4,3,2,1,0:T(8,128)(2,1)} %bitcast.2, bf16[2,32,512]{2,1,0:T(8,128)(2,1)} %constant.14.clone.refs_4_, ...), custom_call_target="tpu_custom_call" | custom-call | tf_op jit(solution)/shard_map/pallas_call | solution.py:300
  20.4 2.1 %shard_map.110 = bf16[128,32,96]{2,1,0:T(8,128)(2,1)} custom-call(bf16[128,32,96]{2,1,0:T(8,128)(2,1)} %shard_map.109.source), custom_call_target="tpu_custom_call" | custom-call | tf_op jit(solution)/shard_map/pallas_call | solution.py:324

commit v7 on v6

--- a/solution.py
+++ b/solution.py
@@ -14,6 +14,7 @@
 MESH = pl.DeviceIdType.MESH
 GROUP = 4
 EDGE = 4
+PARTS = 4
 LIMIT = 60 * 1024 * 1024
 
 
@@ -81,9 +82,9 @@
 
 
 def kernel(nkz, ngx, *refs):
-    sources, out, held = refs[:11], refs[11], refs[12:23]
-    lines, order, table, parts, to_lanes, ky_start, kz_start, to_rows, to_slabs, acquired, to_ky = held
-    near, far, weights, planes, spectra, natural, chosen, staged, load, unload, send_x, recv_x, send_z, recv_z = refs[23:]
+    sources, out, held = refs[:10], refs[10], refs[11:21]
+    lines, order, table, parts, to_lanes, ky_start, kz_start, to_rows, to_slabs, acquired = held
+    near, far, weights, planes, spectra, natural, chosen, load, unload, send_x, recv_x, send_z, recv_z = refs[21:]
     b, g = lax.axis_index("kz"), lax.axis_index("gx")
     barrier = pltpu.get_barrier_semaphore()
     for k in range(1, ngx):
@@ -211,11 +212,10 @@
                 far[pl.ds(base + cells - 1 - a, hx, stride=pitch), :] = piece
 
     each = 128 // cells
-    width = to_ky.shape[1] // each
     step = 2 * each
     odd = lax.broadcasted_iota(jnp.int32, (2 * values, 2 * 128), 0) % 2
     position = jnp.concatenate([acquired[...]] * step, axis=1) - odd
-    batch = chosen.shape[0] // halves
+    batch = chosen.shape[0] // PARTS
     leaving = []
     for h in range(halves):
         regroup(h)
@@ -234,41 +234,47 @@
                 for half in range(2):
                     at = (start // each + half) * 2 * values
                     chosen[at : at + 2 * values, ry * 128 : (ry + 1) * 128] = picked[:, half * 128 : (half + 1) * 128]
-        at = h * batch
-        spread = jnp.dot(chosen[at : at + batch, :], to_ky[...], preferred_element_type=f32).astype(bf16)
-        for row in range(0, batch, 2 * values):
-            for n in range(each):
-                x = (at + row) // (2 * values) * each + n
-                for s in range(2):
-                    first = row + s * values
-                    staged[s * xs + x] = spread[first : first + values, n * width : n * width + 3 * cells]
-        for s in range(2):
-            part = pl.ds(s * xs + h * hx, hx)
-            leaving.append(pltpu.make_async_copy(staged.at[part], out.at[part], unload.at[len(leaving)]))
-            leaving[-1].start()
+            done = (start + step) // each * 2 * values
+            if done % batch == 0:
+                part = pl.ds(done - batch, batch)
+                leaving.append(pltpu.make_async_copy(chosen.at[part], out.at[part], unload.at[len(leaving)]))
+                leaving[-1].start()
     for copy in list(along_x.values()) + list(along_z.values()):
         copy.wait_send()
     for copy in leaving:
         copy.wait()
 
 
-def copy_kernel(source, target, held, entering, leaving):
-    count = entering.shape[0]
-    size = source.shape[0] // count
-    pairs = []
-    for n in range(count):
-        part = pl.ds(n * size, size)
-        pairs.append((
-            pltpu.make_async_copy(source.at[part], held.at[part], entering.at[n]),
-            pltpu.make_async_copy(held.at[part], target.at[part], leaving.at[n]),
-        ))
-    for first, _ in pairs:
-        first.start()
-    for first, second in pairs:
-        first.wait()
-        second.start()
-    for _, second in pairs:
-        second.wait()
+def spread_kernel(xs, cells, chosen, to_ky, out, chosen_held, to_ky_held, staged, entering, leaving):
+    each = 128 // cells
+    width = to_ky.shape[1] // each
+    batch = chosen.shape[0] // PARTS
+    rows = chosen.shape[0] * each // xs
+    values = rows // 2
+    loading = [pltpu.make_async_copy(to_ky, to_ky_held, entering.at[PARTS])]
+    for n in range(PARTS):
+        part = pl.ds(n * batch, batch)
+        loading.append(pltpu.make_async_copy(chosen.at[part], chosen_held.at[part], entering.at[n]))
+    for copy in loading:
+        copy.start()
+    loading[0].wait()
+    stores = []
+    for n in range(PARTS):
+        loading[n + 1].wait()
+        block = chosen_held[n * batch : (n + 1) * batch, :]
+        spread = jnp.dot(block, to_ky_held[...], preferred_element_type=jnp.float32).astype(jnp.bfloat16)
+        for row in range(0, batch, rows):
+            for m in range(each):
+                x = (n * batch + row) // rows * each + m
+                for s in range(2):
+                    first = row + s * values
+                    staged[s * xs + x] = spread[first : first + values, m * width : m * width + 3 * cells]
+        for s in range(2):
+            part = pl.ds(s * xs + n * (xs // PARTS), xs // PARTS)
+            stores.append(pltpu.make_async_copy(staged.at[part], out.at[part], leaving.at[len(stores)]))
+            stores[-1].start()
+    for copy in stores:
+        copy.wait()
 
 
 def local(kspace_lines, acquired_at, ky_start, kz_start, kernels):
@@ -279,8 +285,7 @@
     each = 128 // cells
     width = -(-3 * cells // 128) * 128
     sets = nkz // GROUP
-    halves = 2 if xs % 32 == 0 else 1
-    hx = xs // halves
+    halves, hx = 1, xs
     taps = 10 * 128 * sets
     lattice = pltpu.VMEM((sets * xs * (cells + 2 * EDGE), 128), jnp.float32)
     operands = [
@@ -294,12 +299,11 @@
         jnp.asarray(row_order(coils)),
         jnp.asarray(slab_order(2 * coils)),
         acquired_at,
-        jnp.asarray(lane_order(cells, width)),
     ]
     held = [pltpu.SMEM(o.shape, o.dtype) if o.ndim == 1 else pltpu.VMEM(o.shape, o.dtype) for o in operands]
-    filled = pl.pallas_call(
+    chosen = pl.pallas_call(
         functools.partial(kernel, nkz, ngx),
-        out_shape=jax.ShapeDtypeStruct((2 * xs, 2 * coils, 3 * cells), jnp.bfloat16),
+        out_shape=jax.ShapeDtypeStruct((xs // each * 4 * coils, 3 * 128), jnp.bfloat16),
         in_specs=[pl.BlockSpec(memory_space=pltpu.HBM)] * len(operands),
         out_specs=pl.BlockSpec(memory_space=pltpu.HBM),
         scratch_shapes=held + [
@@ -310,9 +314,8 @@
             pltpu.VMEM((ngx, halves, hx, 128), jnp.bfloat16),
             pltpu.VMEM((14 * coils, taps), jnp.bfloat16),
             pltpu.VMEM((xs // each * 4 * coils, 3 * 128), jnp.bfloat16),
-            pltpu.VMEM((2 * xs, 2 * coils, 3 * cells), jnp.bfloat16),
             pltpu.SemaphoreType.DMA((len(operands),)),
-            pltpu.SemaphoreType.DMA((2 * halves,)),
+            pltpu.SemaphoreType.DMA((PARTS,)),
             pltpu.SemaphoreType.DMA((halves, ngx)),
             pltpu.SemaphoreType.DMA((halves, ngx)),
             pltpu.SemaphoreType.DMA((nkz, halves, ngx // 2)),
@@ -321,18 +324,22 @@
         compiler_params=pltpu.CompilerParams(
             collective_id=0, has_side_effects=True, vmem_limit_bytes=LIMIT),
     )(*operands)
+    to_ky = jnp.asarray(lane_order(cells, width))
+    hbm = pl.BlockSpec(memory_space=pltpu.HBM)
     filled = pl.pallas_call(
-        copy_kernel,
-        out_shape=jax.ShapeDtypeStruct(filled.shape, filled.dtype),
-        in_specs=[pl.BlockSpec(memory_space=pltpu.HBM)],
-        out_specs=pl.BlockSpec(memory_space=pltpu.HBM),
+        functools.partial(spread_kernel, xs, cells),
+        out_shape=jax.ShapeDtypeStruct((2 * xs, 2 * coils, 3 * cells), jnp.bfloat16),
+        in_specs=[hbm, hbm],
+        out_specs=hbm,
         scratch_shapes=[
-            pltpu.VMEM(filled.shape, filled.dtype),
-            pltpu.SemaphoreType.DMA((8,)),
-            pltpu.SemaphoreType.DMA((8,)),
+            pltpu.VMEM(chosen.shape, chosen.dtype),
+            pltpu.VMEM(to_ky.shape, to_ky.dtype),
+            pltpu.VMEM((2 * xs, 2 * coils, 3 * cells), jnp.bfloat16),
+            pltpu.SemaphoreType.DMA((PARTS + 1,)),
+            pltpu.SemaphoreType.DMA((2 * PARTS,)),
         ],
         compiler_params=pltpu.CompilerParams(vmem_limit_bytes=LIMIT),
-    )(filled)
+    )(chosen, to_ky)
     return filled.reshape(2, xs, coils, 2, 3 * cells)
 
 

time: 22.6 us -> 22.9 us (1.013)
  Pallas kernels: 22.4 us -> 22.7 us
    pallas_call x1, Pallas kernels: 2.09 us -> 3.05 us  [local(): pl.pallas_call(functools.partial(spread_kernel, xs, cells), out_shape=jax...]
    pallas_call x1, Pallas kernels: 20.4 us -> 19.7 us  [local(): pl.pallas_call(functools.partial(kernel, nkz, ngx), out_shape=jax.ShapeDt...]
where the time goes in v7:
time: 22.9 us; the launch traced here: 22.7 us
  Pallas kernels  22.7 us (99%)
    pallas_call x1, Pallas kernels, local(): pl.pallas_call(functools.partial(kernel, nkz, ngx), out_shape=jax.ShapeDt...  19.7 us
    pallas_call x1, Pallas kernels, local(): pl.pallas_call(functools.partial(spread_kernel, xs, cells), out_shape=jax...  3.05 us

profile of v7, /device:TPU:0, one launch (start us, length us, event | category | flops | bytes accessed | tf_op | source)
XLA Modules:
  0.0 22.7 jit_solution(6552525431539658608)
XLA Ops:
  0.0 19.7 %shard_map.109.chosen = bf16[1024,384]{1,0:T(8,128)(2,1)} custom-call(bf16[16,1,4,2,512]{4,3,2,1,0:T(2,128)(2,1)} %refs_0_.1, bf16[256,128]{1,0:T(8,128)(2,1)} %constant.12.clone.refs_1_, bf16[512,1024]{1,0:T(8,128)(2,1)} %constant.13.clone.refs_2_, bf16[2,6,6,16,32]{4,3,2,1,0:T(8,128)(2,1)} %bitcast.2, bf16[2,32,512]{2,1,0:T(8,128)(2,1)} %constant.14.clone.refs_4_, ...), custom_call_target="tpu_custom_call" | custom-call | tf_op jit(solution)/shard_map/pallas_call | solution.py:304
  19.7 3.1 %shard_map.110 = bf16[128,32,96]{2,1,0:T(8,128)(2,1)} custom-call(bf16[1024,384]{1,0:T(8,128)(2,1)} %shard_map.109.chosen, bf16[384,512]{1,0:T(8,128)(2,1)} %constant.17.clone.to_ky), custom_call_target="tpu_custom_call" | custom-call | tf_op jit(solution)/shard_map/pallas_call | solution.py:329

commit v8 on v6

--- a/solution.py
+++ b/solution.py
@@ -279,7 +279,7 @@
     each = 128 // cells
     width = -(-3 * cells // 128) * 128
     sets = nkz // GROUP
-    halves = 2 if xs % 32 == 0 else 1
+    halves = 1
     hx = xs // halves
     taps = 10 * 128 * sets
     lattice = pltpu.VMEM((sets * xs * (cells + 2 * EDGE), 128), jnp.float32)

time: 22.6 us -> 22.8 us (level)
  no operation moved by 1% of the time
where the time goes in v8:
time: 22.8 us; the launch traced here: 22.6 us
  Pallas kernels  22.6 us (99%)
    pallas_call x1, Pallas kernels, local(): pl.pallas_call(functools.partial(kernel, nkz, ngx), out_shape=jax.ShapeDt...  20.5 us
    pallas_call x1, Pallas kernels, local(): pl.pallas_call(copy_kernel, out_shape=jax.ShapeDtypeStruct(filled.shape,...  2.09 us

profile of v8, /device:TPU:0, one launch (start us, length us, event | category | flops | bytes accessed | tf_op | source)
XLA Modules:
  0.0 22.6 jit_solution(17024422992942515432)
XLA Ops:
  0.0 20.5 %shard_map.109.source = bf16[128,32,96]{2,1,0:T(8,128)(2,1)} custom-call(bf16[16,1,4,2,512]{4,3,2,1,0:T(2,128)(2,1)} %refs_0_.1, bf16[256,128]{1,0:T(8,128)(2,1)} %constant.12.clone.refs_1_, bf16[512,1024]{1,0:T(8,128)(2,1)} %constant.13.clone.refs_2_, bf16[2,6,6,16,32]{4,3,2,1,0:T(8,128)(2,1)} %bitcast.2, bf16[2,32,512]{2,1,0:T(8,128)(2,1)} %constant.14.clone.refs_4_, ...), custom_call_target="tpu_custom_call" | custom-call | tf_op jit(solution)/shard_map/pallas_call | solution.py:300
  20.5 2.1 %shard_map.110 = bf16[128,32,96]{2,1,0:T(8,128)(2,1)} custom-call(bf16[128,32,96]{2,1,0:T(8,128)(2,1)} %shard_map.109.source), custom_call_target="tpu_custom_call" | custom-call | tf_op jit(solution)/shard_map/pallas_call | solution.py:324
